TPU v7x, 512 devices: a whole 4x4x16 slice. The times are simulated.
512 devices in a mesh: tok: 16 (over y, x), hid: 8 (over z_lo, core), ffn: 4 (over z_hi).
Axes of the slice: x: 4, y: 4, z: 16 (z_hi: 4, z_lo: 4; z = z_hi * 4 + z_lo), core: 2. Of those that a mesh axis runs over, the one named last changes fastest.
Arguments:
- tokens: bfloat16 [4096, 5120], P('tok', 'hid'), may hold values from -6 to 6
- gate_weight: bfloat16 [5120, 4096], P('hid', ('ffn', 'tok')), may hold values from -0.078125 to 0.078125
- up_weight: bfloat16 [5120, 4096], P('hid', ('ffn', 'tok')), may hold values from -0.078125 to 0.078125
- down_weight: bfloat16 [4096, 5120], P('ffn', 'hid'), may hold values from -0.09375 to 0.09375
- gate_mask: int32 [40, 32], replicated, may hold values 0 or 1
- up_mask: int32 [40, 32], replicated, may hold values 0 or 1
- down_mask: int32 [32, 40], replicated, may hold values 0 or 1
- cotangent: bfloat16 [4096, 5120], P(('tok', 'ffn'), 'hid'), may hold values from -6 to 6
Outputs:
- mixed: bfloat16 [4096, 5120], P(('tok', 'ffn'), 'hid')
- tokens_grad: bfloat16 [4096, 5120], P('tok', 'hid')
- gate_grad: bfloat16 [5120, 4096], P('hid', ('ffn', 'tok'))
- up_grad: bfloat16 [5120, 4096], P('hid', ('ffn', 'tok'))
- down_grad: bfloat16 [4096, 5120], P(('ffn', 'tok'), 'hid')
All inputs are finite; a program needn't handle non-finite values.
Results may differ from a plain program's by a relative error of at most 0.018.
Values may be sent and summed in bfloat16 or wider, within the bound.
No kernel may reach another device: no remote copies, remote signals or barrier semaphores. Data moves between devices by JAX's collectives and lax.ppermute only.
A program may use at most 64 MiB of HBM per device.

v0:
```python
import jax
import jax.numpy as jnp
from jax import lax
from jax.sharding import PartitionSpec as P

BLOCK = 128


def expand_local(blocks, row_first, row_count, col_first, col_count):
    row_block = (row_first + lax.iota(jnp.int32, row_count)) // BLOCK
    col_block = (col_first + lax.iota(jnp.int32, col_count)) // BLOCK
    row_select = (row_block[:, None] == lax.iota(jnp.int32, blocks.shape[0])[None, :]).astype(
        jnp.float32
    )
    col_select = (lax.iota(jnp.int32, blocks.shape[1])[:, None] == col_block[None, :]).astype(
        jnp.float32
    )
    inner = jnp.dot(row_select, blocks.astype(jnp.float32), precision=lax.Precision.HIGHEST)
    return jnp.dot(inner, col_select, precision=lax.Precision.HIGHEST).astype(jnp.bfloat16)


def contract_rows(left, right):
    return lax.dot_general(
        left, right, (((0,), (0,)), ((), ())), preferred_element_type=jnp.float32
    )


def contract_cols(left, right):
    return lax.dot_general(
        left, right, (((1,), (1,)), ((), ())), preferred_element_type=jnp.float32
    )


def body(tokens, gate_weight, up_weight, down_weight, gate_mask, up_mask, down_mask, cotangent):
    feature_count = tokens.shape[1]
    unit_count = down_weight.shape[0]
    feature_first = lax.axis_index("hid") * feature_count
    unit_first = lax.axis_index("ffn") * unit_count
    group_scale = 1.0 / lax.axis_size("tok")
    keep_gate = expand_local(gate_mask, feature_first, feature_count, unit_first, unit_count)
    keep_up = expand_local(up_mask, feature_first, feature_count, unit_first, unit_count)
    keep_down = expand_local(down_mask, unit_first, unit_count, feature_first, feature_count)
    down_eff = down_weight * keep_down
    full_gate, full_up = (
        lax.all_gather(gate_weight, "tok", axis=1, tiled=True),
        lax.all_gather(up_weight, "tok", axis=1, tiled=True),
    )
    gate_eff = full_gate * keep_gate
    up_eff = full_up * keep_up
    gate_part = jnp.dot(tokens, gate_eff, preferred_element_type=jnp.float32)
    up_part = jnp.dot(tokens, up_eff, preferred_element_type=jnp.float32)
    gate, up = lax.psum((gate_part, up_part), "hid")
    hidden = (jax.nn.silu(gate) * up).astype(jnp.bfloat16)
    out_term = jnp.dot(hidden, down_eff, preferred_element_type=jnp.float32)
    mixed = lax.psum_scatter(out_term.astype(jnp.bfloat16), "ffn", scatter_dimension=0, tiled=True)
    grad_rows = lax.all_gather(cotangent, "ffn", axis=0, tiled=True)
    hidden_grad = lax.psum(contract_cols(grad_rows, down_eff), "hid")
    sigma = jax.nn.sigmoid(gate)
    gate_delta = (hidden_grad * up * sigma * (1.0 + gate * (1.0 - sigma))).astype(jnp.bfloat16)
    up_delta = (hidden_grad * gate * sigma).astype(jnp.bfloat16)
    gate_term = contract_rows(tokens, gate_delta) * keep_gate.astype(jnp.float32)
    up_term = contract_rows(tokens, up_delta) * keep_up.astype(jnp.float32)
    gate_sum, up_sum = (
        lax.psum_scatter(
            gate_term.astype(jnp.bfloat16), "tok", scatter_dimension=1, tiled=True
        ).astype(jnp.float32),
        lax.psum_scatter(
            up_term.astype(jnp.bfloat16), "tok", scatter_dimension=1, tiled=True
        ).astype(jnp.float32),
    )
    down_term = contract_rows(hidden, grad_rows) * keep_down.astype(jnp.float32)
    down_sum = lax.psum_scatter(
        down_term.astype(jnp.bfloat16), "tok", scatter_dimension=0, tiled=True
    ).astype(jnp.float32)
    input_part = contract_cols(gate_delta, gate_eff) + contract_cols(up_delta, up_eff)
    tokens_grad = lax.psum(input_part, "ffn").astype(jnp.bfloat16)
    gate_out = (gate_sum * group_scale).astype(jnp.bfloat16)
    up_out = (up_sum * group_scale).astype(jnp.bfloat16)
    down_out = (down_sum * group_scale).astype(jnp.bfloat16)
    return (mixed, tokens_grad, gate_out, up_out, down_out)


def solution(mesh):
    in_specs = (
        P("tok", "hid"),
        P("hid", ("ffn", "tok")),
        P("hid", ("ffn", "tok")),
        P("ffn", "hid"),
        P(),
        P(),
        P(),
        P(("tok", "ffn"), "hid"),
    )
    out_specs = (
        P(("tok", "ffn"), "hid"),
        P("tok", "hid"),
        P("hid", ("ffn", "tok")),
        P("hid", ("ffn", "tok")),
        P(("ffn", "tok"), "hid"),
    )
    return jax.shard_map(body, mesh=mesh, in_specs=in_specs, out_specs=out_specs, check_vma=False)
```

profile of v0, /device:TPU:1, one launch (start us, length us, event | category | flops | bytes accessed | tf_op | source)
XLA Modules:
  0.0 571.0 jit_solution(7108524246870963148)
XLA Ops:
  7.2 0.0 all-gather.3.cloned.1.call-start
  7.2 0.7 all-gather.3.cloned.1.call-update
  7.9 0.0 all-gather.5.cloned.1.call-start
  8.0 0.7 all-gather.5.cloned.1.call-update
  8.7 0.0 all-reduce.4.cloned.1.call-start
  8.8 25.7 %all_gather.11 = bf16[256,640]{1,0:T(8,128)(2,1)S(1)} all-gather(bf16[64,640]{1,0:T(8,128)(2,1)} %param.15), channel_id=1, replica_groups=mesh['tok'=16,'hid'=8,'ffn'=4] {'ffn'}, dimensions={0}, use_global_device_ids=true | all-gather | bytes 409600 | tf_op jit(solution)/shard_map/all_gather | solution.py:56
  34.5 1.1 fusion.7
  35.6 1.1 fusion.8
  36.7 1.2 fusion.2
  37.8 1.2 convolution_convert_fusion
  39.0 1.2 convolution_convert_fusion.2
  40.2 0.1 copy-done.4
  40.3 1.6 convolution_bitcast_fusion
  42.0 32.2 %all-gather.3.cloned.1.call-done = bf16[640,1024]{0,1:T(8,128)(2,1)} async-done(((bf16[640,64]{0,1:T(8,128)(2,1)}), bf16[640,1024]{0,1:T(8,128)(2,1)}) %all-gather.3.cloned.1.call-update) | async-done | bytes 1310736 | tf_op jit(solution)/shard_map/all_gather | solution.py:45
  74.2 2.5 copy.19
  76.7 3.6 fusion.24
  80.3 1.1 copy-done.1
  81.4 1.6 convolution_bitcast_fusion.2
  83.0 52.4 %all-gather.5.cloned.1.call-done = bf16[640,1024]{0,1:T(8,128)(2,1)} async-done(((bf16[640,64]{0,1:T(8,128)(2,1)}), bf16[640,1024]{0,1:T(8,128)(2,1)}) %all-gather.5.cloned.1.call-update) | async-done | bytes 1310736 | tf_op jit(solution)/shard_map/all_gather | solution.py:46
  135.4 2.5 copy.20
  137.8 3.0 convolution_bitcast_fusion.1
  140.8 0.0 reduce-scatter.13.cloned.1.call-start
  140.9 101.4 %all-reduce.4.cloned.1.call-done = (f32[256,1024]{0,1:T(8,128)}, f32[256,1024]{0,1:T(8,128)}, f32[256,1024]{0,1:T(8,128)}) async-done(((f32[256,1024]{0,1:T(8,128)}, f32[256,1024]{0,1:T(8,128)}, f32[256,1024]{0,1:T(8,128)}), (f32[256,1024]{0,1:T(8,128)}, f32[256,1024]{0,1:T(8,128)}, f32[256,1024]{0,1:T(8,128)})) %all-reduce.4.cloned.1.call-update) | async-done | bytes 3145744 | tf_op jit(solution)/shard_map/psum | solution.py:52
  242.3 3.3 multiply_convert_fusion.1
  245.6 0.8 copy-done.6
  246.4 1.6 fusion.1
  248.0 2.4 copy.27
  250.5 0.0 reduce-scatter.13.cloned.1.call-update
  250.5 0.0 reduce-scatter.15.cloned.1.call-start
  250.5 1.7 fusion
  252.2 2.4 copy.29
  254.6 0.0 reduce-scatter.15.cloned.1.call-update
  254.7 0.0 reduce-scatter.11.cloned.1.call-start
  254.7 2.8 multiply_convert_fusion
  257.6 0.0 reduce-scatter.9.cloned.1.call-start
  257.6 2.2 fusion.25
  259.9 1.6 convolution_add_fusion
  261.4 1.4 convolution_convert_fusion.3
  262.8 61.1 %all-reduce.5 = bf16[256,640]{1,0:T(8,128)(2,1)} all-reduce(f32[256,640]{1,0:T(8,128)S(1)} %copy-done.9), channel_id=1, replica_groups=mesh['tok'=16,'hid'=8,'ffn'=4] {'ffn'}, use_global_device_ids=true, to_apply=%region_4.5 | all-reduce | flops 163840 | bytes 983040 | tf_op jit(solution)/shard_map/psum | solution.py:76
  323.9 13.7 %reduce-scatter.13.cloned.1.call-done = bf16[64,640]{1,0:T(8,128)(2,1)} async-done(((bf16[1024,640]{1,0:T(8,128)(2,1)}), bf16[64,640]{1,0:T(8,128)(2,1)}) %reduce-scatter.13.cloned.1.call-update) | async-done | bytes 81936
  337.6 1.0 copy.28
  338.7 0.8 copy.23
  339.5 90.1 %reduce-scatter.15.cloned.1.call-done = bf16[64,640]{1,0:T(8,128)(2,1)} async-done(((bf16[1024,640]{1,0:T(8,128)(2,1)}), bf16[64,640]{1,0:T(8,128)(2,1)}) %reduce-scatter.15.cloned.1.call-update) | async-done | bytes 81936
  429.6 1.0 copy.30
  430.7 0.8 copy.24
  431.4 90.1 %reduce-scatter.11.cloned.1.call-done = bf16[64,640]{1,0:T(8,128)(2,1)} async-done(((bf16[1024,640]{1,0:T(8,128)(2,1)}), bf16[64,640]{1,0:T(8,128)(2,1)}) %reduce-scatter.11.cloned.1.call-update) | async-done | bytes 81936 | tf_op jit(solution)/shard_map/reduce_scatter | solution.py:72
  521.5 1.5 multiply_convert_fusion.6
  523.1 41.1 %reduce-scatter.9.cloned.1.call-done = bf16[64,640]{1,0:T(8,128)(2,1)} async-done(((bf16[256,640]{1,0:T(8,128)(2,1)}), bf16[64,640]{1,0:T(8,128)(2,1)}) %reduce-scatter.9.cloned.1.call-update) | async-done | bytes 81936 | tf_op jit(solution)/shard_map/reduce_scatter | solution.py:55
  (24 shorter events, 0.2 us)
Async XLA Ops:
  7.2 74.2 %copy-start = (bf16[256,640]{1,0:T(8,128)(2,1)S(1)}, bf16[256,640]{1,0:T(8,128)(2,1)}, u32[]{:S(2)}) copy-start(bf16[256,640]{1,0:T(8,128)(2,1)} %param.8) | copy-start | bytes 983044
  7.2 67.0 %all-gather.3.cloned.1.call-start = ((), (), s32[]{:S(2)}) async-start(), calls=%async_computation.4 | async-start | bytes 1392640 | tf_op jit(solution)/shard_map/all_gather | solution.py:45
  7.9 127.5 %all-gather.5.cloned.1.call-start = ((), (), s32[]{:S(2)}) async-start(), calls=%async_computation.5 | async-start | bytes 1392640 | tf_op jit(solution)/shard_map/all_gather | solution.py:46
  8.7 233.6 %all-reduce.4.cloned.1.call-start = ((), (), s32[]{:S(2)}) async-start(), calls=%async_computation.10 | async-start | bytes 6291456 | tf_op jit(solution)/shard_map/psum | solution.py:52
  34.5 5.7 %copy-start.8 = (bf16[256,640]{1,0:T(8,128)(2,1)}, bf16[256,640]{1,0:T(8,128)(2,1)S(1)}, u32[]{:S(2)}) copy-start(bf16[256,640]{1,0:T(8,128)(2,1)S(1)} %all_gather.11) | copy-start | bytes 983044
  39.0 1.3 copy-start.4
  80.3 1.1 copy-start.1
  140.8 196.8 %reduce-scatter.13.cloned.1.call-start = ((), (), s32[]{:S(2)}) async-start(), calls=%async_computation.8 | async-start | bytes 1392640
  242.3 4.1 copy-start.3
  245.6 0.8 copy-start.6
  250.5 179.1 %reduce-scatter.15.cloned.1.call-start = ((), (), s32[]{:S(2)}) async-start(), calls=%async_computation.9 | async-start | bytes 1392640
  254.7 266.9 %reduce-scatter.11.cloned.1.call-start = ((), (), s32[]{:S(2)}) async-start(), calls=%async_computation.7 | async-start | bytes 1392640 | tf_op jit(solution)/shard_map/reduce_scatter | solution.py:72
  257.6 306.6 %reduce-scatter.9.cloned.1.call-start = ((), (), s32[]{:S(2)}) async-start(), calls=%async_computation.6 | async-start | bytes 409600 | tf_op jit(solution)/shard_map/reduce_scatter | solution.py:55
  257.6 2.2 copy-start.2
  259.8 1.6 copy-start.5
  259.8 1.6 copy-start.7
  261.4 1.4 copy-start.9
Sparse Core Ops, SparseCore 0:
  11.0 63.1 all-gather.2
  77.2 58.1 all-gather.4
  141.0 101.2 all-reduce.3
  250.6 86.9 reduce-scatter.12
  341.5 87.9 reduce-scatter.14
  433.5 87.9 reduce-scatter.10
  524.9 39.1 reduce-scatter.8
where the time goes:
time: 572 us; the launch traced here: 571 us
  waiting for transfers between devices  422 us (74%)
  blocking collectives  86.8 us (15%)
  matrix products  26.7 us (5%)
  local copies, waits for them, and re-layouts  15.5 us (3%)
  between operations  14.3 us (2%)
    unnamed x9, waiting for transfers between devices  105 us
    psum x1, waiting for transfers between devices, body(): gate, up = lax.psum((gate_part, up_part), 'hid')  101 us
    reduce_scatter x1, waiting for transfers between devices, body(): lax.psum_scatter(down_term.astype(jnp.bfloat16), 'tok', scatter_dimension...  90.1 us
    psum x1, blocking collectives, body(): tokens_grad = lax.psum(input_part, 'ffn').astype(jnp.bfloat16)  61.1 us
    all_gather x1, waiting for transfers between devices, body(): lax.all_gather(up_weight, 'tok', axis=1, tiled=True)  52.4 us
    reduce_scatter x1, waiting for transfers between devices, body(): lax.psum_scatter(out_term.astype(jnp.bfloat16), 'ffn', scatter_dimension=...  41.1 us
    all_gather x1, waiting for transfers between devices, body(): lax.all_gather(gate_weight, 'tok', axis=1, tiled=True)  32.2 us
    all_gather x1, blocking collectives, body(): grad_rows = lax.all_gather(cotangent, 'ffn', axis=0, tiled=True)  25.7 us
  transfers between devices with their start and end apart: 7, of which 7 were waited for; matrix products, arithmetic and copies ran while one was open for 6% of the time, Pallas kernels for 0%

commit v1 on v0

v1 whole, which is shorter than its diff:
```python
import jax
import jax.numpy as jnp
from jax import lax
from jax.experimental import pallas as pl
from jax.experimental.pallas import tpu as pltpu
from jax.sharding import PartitionSpec as P

BLOCK = 128
BF = jnp.bfloat16
F32 = jnp.float32
CHIPS_Y = 4


def dot(left, right, left_axis, right_axis):
    return lax.dot_general(
        left, right, (((left_axis,), (right_axis,)), ((), ())), preferred_element_type=F32
    )


def total(parts):
    return jnp.sum(parts.astype(F32), axis=0)


def pick(parts, index):
    return lax.dynamic_index_in_dim(parts, index, 0, keepdims=False)


def keep_rows(mask, row_first, row_blocks, col_first, col_blocks):
    part = lax.dynamic_slice(mask, (row_first, col_first), (row_blocks, col_blocks))
    return jnp.repeat(part.astype(BF), BLOCK, axis=1)


def activation_kernel(own, units, part_ref, out_ref):
    for k in range(units // own):
        at = 2 * own * k
        gate = total(part_ref[:, :, at : at + own])
        up = total(part_ref[:, :, at + own : at + 2 * own])
        hidden_grad = total(part_ref[:, :, 2 * units + own * k : 2 * units + own * (k + 1)])
        sigma = jax.nn.sigmoid(gate)
        out_ref[:, 2 * units + own * k : 2 * units + own * (k + 1)] = (gate * sigma * up).astype(BF)
        out_ref[:, at : at + own] = (
            hidden_grad * up * sigma * (1.0 + gate * (1.0 - sigma))
        ).astype(BF)
        out_ref[:, at + own : at + 2 * own] = (hidden_grad * gate * sigma).astype(BF)


def activation(own, units, parts):
    count = parts.shape[1]
    return pl.pallas_call(
        lambda *refs: activation_kernel(own, units, *refs),
        out_shape=jax.ShapeDtypeStruct((count, 3 * units), BF),
        in_specs=[pl.BlockSpec(memory_space=pltpu.VMEM)],
        out_specs=pl.BlockSpec(memory_space=pltpu.VMEM),
        compiler_params=pltpu.CompilerParams(vmem_limit_bytes=16 * 2**20),
        cost_estimate=pl.CostEstimate(
            flops=20 * count * units, bytes_accessed=30 * count * units, transcendentals=count * units
        ),
    )(parts)


def body(tokens, gate_weight, up_weight, down_weight, gate_mask, up_mask, down_mask, cotangent):
    n_tok, n_hid, n_ffn = (lax.axis_size(a) for a in ("tok", "hid", "ffn"))
    t, h, f = (lax.axis_index(a) for a in ("tok", "hid", "ffn"))
    rows, feats = tokens.shape
    units = down_weight.shape[0]
    own = units // n_tok
    feat_blocks, unit_blocks = feats // BLOCK, units // BLOCK
    n_line = n_hid // 2
    c = h % 2
    n_y = CHIPS_Y
    n_x = n_tok // n_y
    pairs = [[2 * i + j for j in range(2)] for i in range(n_line)]
    lines = [[2 * i + j for i in range(n_line)] for j in range(2)]
    along_y = [[n_x * i + j for i in range(n_y)] for j in range(n_x)]
    along_x = [[n_x * i + j for j in range(n_x)] for i in range(n_y)]

    def hop_hid(value, distance):
        return lax.ppermute(value, "hid", [(i, i ^ distance) for i in range(n_hid)])

    own_block = (f * units + t * own) // BLOCK
    keep_gate = keep_rows(gate_mask.T, own_block, 1, h * feat_blocks, feat_blocks)
    keep_up = keep_rows(up_mask.T, own_block, 1, h * feat_blocks, feat_blocks)
    keep_own_down = keep_rows(down_mask, own_block, 1, h * feat_blocks, feat_blocks)
    keep_down = keep_rows(down_mask, f * unit_blocks, unit_blocks, h * feat_blocks, feat_blocks)
    down_eff = (down_weight.reshape(unit_blocks, BLOCK, feats) * keep_down[:, None, :]).reshape(
        units, feats
    )

    is_gate = lax.broadcasted_iota(jnp.int32, (n_tok, 2, own, feats), 1) == 0
    spread = jnp.where(is_gate, (gate_weight.T * keep_gate)[None, None], (up_weight.T * keep_up)[None, None])
    spread = spread.reshape(n_tok, 2 * own, feats)
    weights = lax.all_to_all(spread, "tok", 0, 0).reshape(2 * units, feats)
    grad_rows = lax.all_gather(cotangent, "ffn", axis=0, tiled=True)

    def gather_y(array):
        return lax.all_gather(array, "tok", axis=0, tiled=True, axis_index_groups=along_y)

    tokens_y = gather_y(tokens)

    def sum_cores(part):
        part = part.astype(BF).reshape(2, rows // 2, part.shape[1])
        half = pick(part, c).astype(F32) + hop_hid(pick(part, 1 - c), 1).astype(F32)
        return half.astype(BF).reshape(n_line, rows // n_hid, part.shape[2])

    grad_half = sum_cores(dot(grad_rows, down_eff, 1, 1))
    weights, grad_half = lax.optimization_barrier((weights, grad_half))
    both_half = sum_cores(dot(tokens, weights, 1, 1))
    parts = lax.all_to_all(
        jnp.concatenate([both_half, grad_half], axis=2), "hid", 0, 0, axis_index_groups=lines
    )
    acts = activation(own, units, parts)
    mine = lax.all_gather(acts, "hid", axis=0, tiled=True, axis_index_groups=lines)
    mine, tokens_y = lax.optimization_barrier((mine, tokens_y))
    other = hop_hid(mine, 1)

    def in_order(first, last):
        halves = mine[:, first:last], other[:, first:last]
        return jnp.concatenate([jnp.where(c == k, *halves) for k in range(2)])

    deltas = in_order(0, 2 * units)
    hidden = in_order(2 * units, 3 * units)

    def exchange(parts, groups=None):
        return lax.all_to_all(parts, "tok", 0, 0, axis_index_groups=groups)

    quarter = deltas.reshape(rows, n_y, 2 * units // n_y).transpose(1, 0, 2)
    quarter = exchange(quarter, along_y).reshape(n_y * rows, 2 * units // n_y)

    def beside(i):
        return i ^ 1

    def around(i):
        return n_ffn - 1 - i

    def swap(values, pairing):
        sent = jnp.concatenate(values)
        return lax.ppermute(sent, "ffn", [(i, pairing(i)) for i in range(n_ffn)])

    def plus(left, right):
        return (left.astype(F32) + right.astype(F32)).astype(BF)

    input_part = dot(deltas, weights, 1, 0).astype(BF).reshape(2, rows // 2, feats)
    mixed_part = dot(hidden, down_eff, 1, 0).astype(BF)
    mixed_part = mixed_part.reshape(n_ffn, 2, rows // n_ffn // 2, feats)
    half, block = rows // 2, rows // n_ffn // 2
    pairings = ((beside, around), (around, beside))
    waiting = []
    for k, (first, second) in enumerate(pairings):
        piece = mixed_part[:, k]
        got = swap([input_part[k], pick(piece, first(f)), pick(piece, second(first(f)))], first)
        waiting.append(
            (
                plus(input_part[k], got[:half]),
                plus(pick(piece, f), got[half : half + block]),
                plus(pick(piece, second(f)), got[half + block :]),
            )
        )
    waiting, quarter = lax.optimization_barrier((waiting, quarter))
    input_sums, mixed_sums = [], []
    for (first, second), (input_sum, own_sum, sent_sum) in zip(pairings, waiting):
        got = swap([input_sum, sent_sum], second)
        input_sums.append(plus(input_sum, got[:half]))
        mixed_sums.append(plus(own_sum, got[half:]))
    tokens_grad = jnp.concatenate(input_sums)
    mixed = jnp.concatenate(mixed_sums)

    down_term = dot(hidden, grad_rows, 0, 0).astype(BF).reshape(n_tok, own, feats)
    down_sum = total(exchange(down_term)) * (1.0 / n_tok)
    delta_term = dot(quarter, tokens_y, 0, 0).astype(BF).reshape(n_x, 2 * own, feats)
    sums = total(exchange(delta_term, along_x)) * (1.0 / n_tok)
    gate_grad = (sums[:own] * keep_gate.astype(F32)).astype(BF).T
    up_grad = (sums[own:] * keep_up.astype(F32)).astype(BF).T
    down_grad = (down_sum * keep_own_down.astype(F32)).astype(BF)
    return (mixed, tokens_grad, gate_grad, up_grad, down_grad)


def solution(mesh):
    in_specs = (
        P("tok", "hid"),
        P("hid", ("ffn", "tok")),
        P("hid", ("ffn", "tok")),
        P("ffn", "hid"),
        P(),
        P(),
        P(),
        P(("tok", "ffn"), "hid"),
    )
    out_specs = (
        P(("tok", "ffn"), "hid"),
        P("tok", "hid"),
        P("hid", ("ffn", "tok")),
        P("hid", ("ffn", "tok")),
        P(("ffn", "tok"), "hid"),
    )
    return jax.shard_map(body, mesh=mesh, in_specs=in_specs, out_specs=out_specs, check_vma=False)
```

time: 572 us -> 210 us (0.37)
  waiting for transfers between devices: 422 us -> 54.9 us
  starting transfers between devices: 0.28 us -> 66.5 us
  blocking collectives: 86.8 us -> 39.9 us
  matrix products: 26.7 us -> 10.4 us
  other arithmetic: 4.96 us -> 18.1 us
  local copies, waits for them, and re-layouts: 15.5 us -> 2.71 us
    reduce_scatter x2 -> x0, waiting for transfers between devices: 131 us -> none  [the longest x1 90.1 us: body(): lax.psum_scatter(down_term.astype(jnp.bfloat16), 'tok', scatter_dimension...]
    unnamed x9 -> x1, waiting for transfers between devices: 105 us -> 0.71 us
    psum x1 -> x0, waiting for transfers between devices: 101 us -> none  [body(): gate, up = lax.psum((gate_part, up_part), 'hid')]
    all_gather x2 -> x1, waiting for transfers between devices: 84.6 us -> 0.01 us  [gather_y(): lax.all_gather(array, 'tok', axis=0, tiled=True, axis_index_groups=along_y)]
    psum x1 -> x0, blocking collectives: 61.1 us -> none  [body(): tokens_grad = lax.psum(input_part, 'ffn').astype(jnp.bfloat16)]
    ppermute x0 -> x7, starting transfers between devices: none -> 39.7 us  [the longest x4 26.4 us: swap(): return lax.ppermute(sent, 'ffn', [(i, pairing(i)) for i in range(n_ffn)])]
    ppermute x0 -> x7, waiting for transfers between devices: none -> 27.4 us  [the longest x4 23.4 us: swap(): return lax.ppermute(sent, 'ffn', [(i, pairing(i)) for i in range(n_ffn)])]
    all_to_all x0 -> x5, starting transfers between devices: none -> 26.8 us  [the longest x3 11.6 us: exchange(): return lax.all_to_all(parts, 'tok', 0, 0, axis_index_groups=groups)]
  transfers between devices with their start and end apart: 7 -> 13, of which waited for: 7 -> 8; matrix products, arithmetic and copies ran while one was open for 6% -> 8% of each run, Pallas kernels for 0% -> 0%
where the time goes in v1:
time: 210 us; the launch traced here: 208 us
  starting transfers between devices  66.5 us (32%)
  waiting for transfers between devices  54.9 us (26%)
  blocking collectives  39.9 us (19%)
  other arithmetic  18.1 us (9%)
  between operations  14.5 us (7%)
  matrix products  10.4 us (5%)
  local copies, waits for them, and re-layouts  2.71 us (1%)
    ppermute x4, starting transfers between devices, swap(): return lax.ppermute(sent, 'ffn', [(i, pairing(i)) for i in range(n_ffn)])  26.4 us
    all_gather x1, blocking collectives, body(): grad_rows = lax.all_gather(cotangent, 'ffn', axis=0, tiled=True)  24.4 us
    ppermute x4, waiting for transfers between devices, swap(): return lax.ppermute(sent, 'ffn', [(i, pairing(i)) for i in range(n_ffn)])  23.4 us
    all_to_all x1, waiting for transfers between devices, body(): lax.all_to_all(jnp.concatenate([both_half, grad_half], axis=2), 'hid', 0,...  18.9 us
    all_gather x1, blocking collectives, body(): lax.all_gather(acts, 'hid', axis=0, tiled=True, axis_index_groups=lines)  15.5 us
    ppermute x3, starting transfers between devices, hop_hid(): return lax.ppermute(value, 'hid', [(i, i ^ distance) for i in range(n_hid)])  13.3 us
    all_to_all x3, starting transfers between devices, exchange(): return lax.all_to_all(parts, 'tok', 0, 0, axis_index_groups=groups)  11.6 us
    dot_general x6, matrix products, dot(): lax.dot_general(left, right, (((left_axis,), (right_axis,)), ((), ())), p...  10.4 us
  transfers between devices with their start and end apart: 13, of which 8 were waited for; matrix products, arithmetic and copies ran while one was open for 8% of the time, Pallas kernels for 0%

profile of v1, /device:TPU:1, one launch (start us, length us, event | category | flops | bytes accessed | tf_op | source)
XLA Modules:
  0.0 207.9 jit_solution(744472599517888853)
XLA Ops:
  7.4 0.8 convert_bitcast_fusion
  8.3 0.9 multiply_bitcast_fusion
  9.2 0.9 multiply_bitcast_fusion.1
  10.1 1.8 broadcast_select_fusion
  11.9 7.6 %all-to-all-start = ((bf16[16,128,640]{2,1,0:T(8,128)(2,1)}), bf16[16,128,640]{2,1,0:T(8,128)(2,1)S(1)}, u32[]{:S(2)}, u32[]{:S(2)}) async-start(bf16[16,128,640]{2,1,0:T(8,128)(2,1)} %broadcast_select_fusion), calls=%async_computation | async-start | bytes 5242880 | tf_op jit(solution)/shard_map/all_to_all | solution.py:92
  19.6 0.8 dynamic-slice_convert_fusion
  20.5 2.5 %bitcast_multiply_fusion = bf16[1024,640]{1,0:T(8,128)(2,1)} fusion(bf16[1024,640]{1,0:T(8,128)(2,1)} %param.11, bf16[8,640]{1,0:T(8,128)(2,1)S(1)} %broadcast_bitcast_fusion), kind=kLoop, calls=%fused_computation.5 | loop fusion | flops 655360 | bytes 2631680 | tf_op jit(solution)/shard_map/mul | solution.py:85
  23.1 24.4 %all_gather.9 = bf16[256,640]{1,0:T(8,128)(2,1)S(1)} all-gather(bf16[64,640]{1,0:T(8,128)(2,1)S(1)} %copy-done.7), channel_id=1, replica_groups=mesh['tok'=16,'hid'=8,'ffn'=4] {'ffn'}, dimensions={0}, use_global_device_ids=true | all-gather | bytes 409600 | tf_op jit(solution)/shard_map/all_gather | solution.py:93
  47.5 0.7 copy-done.3
  48.2 1.9 convolution_convert_fusion.3
  50.2 5.5 %collective-permute-start = (bf16[128,1024]{1,0:T(8,128)(2,1)S(1)}, bf16[128,1024]{1,0:T(8,128)(2,1)}, u32[]{:S(2)}, u32[]{:S(2)}) collective-permute-start(bf16[128,1024]{1,0:T(8,128)(2,1)S(1)} %dynamic-slice_bitcast_fusion.1), channel_id=1, source_target_pairs={{0,4},{4,0},{8,12},{12,8},{16,20},{20,16},{24,28},{28,24},{1,5},{5... | collective-permute-start | bytes 786440 | tf_op jit(solution)/shard_map/ppermute | solution.py:78
  55.6 1.3 collective-permute-done
  56.9 1.0 fusion.1
  57.9 2.0 convolution_convert_fusion
  60.0 2.3 %collective-permute-start.1 = (bf16[128,2048]{1,0:T(8,128)(2,1)S(1)}, bf16[128,2048]{1,0:T(8,128)(2,1)S(1)}, u32[]{:S(2)}, u32[]{:S(2)}) collective-permute-start(bf16[128,2048]{1,0:T(8,128)(2,1)S(1)} %dynamic-slice_bitcast_fusion), channel_id=1, source_target_pairs={{0,4},{4,0},{8,12},{12,8},{16,20},{20,16},{24,28},{28,24},{1,5},{5... | collective-permute-start | bytes 1572872 | tf_op jit(solution)/shard_map/ppermute | solution.py:78
  62.3 1.5 collective-permute-done.1
  63.9 0.9 pad_maximum_fusion.1
  64.9 7.6 %all-to-all-start.1 = ((bf16[4,32,3072]{2,1,0:T(8,128)(2,1)}), bf16[4,32,3072]{2,1,0:T(8,128)(2,1)S(1)}, u32[]{:S(2)}, u32[]{:S(2)}) async-start(bf16[4,32,3072]{2,1,0:T(8,128)(2,1)} %pad_maximum_fusion.1), calls=%async_computation.1 | async-start | bytes 1572864 | tf_op jit(solution)/shard_map/all_to_all | solution.py:108
  72.4 0.7 all-gather.2.cloned.1.call-update
  73.1 18.9 %all-to-all-done.1.refs_0_ = bf16[4,32,3072]{2,1,0:T(8,128)(2,1)S(1)} async-done(((bf16[4,32,3072]{2,1,0:T(8,128)(2,1)}), bf16[4,32,3072]{2,1,0:T(8,128)(2,1)S(1)}, u32[]{:S(2)}, u32[]{:S(2)}) %all-to-all-start.1) | async-done | bytes 786464 | tf_op jit(solution)/shard_map/all_to_all | solution.py:108
  92.1 0.9 shard_map.119
  93.0 15.5 %all_gather.10 = bf16[128,3072]{1,0:T(8,128)(2,1)S(1)} all-gather(bf16[32,3072]{1,0:T(8,128)(2,1)S(1)} %shard_map.119), channel_id=1, replica_groups={{0,8,16,24},{4,12,20,28},{1,9,17,25},{5,13,21,29},{2,10,18,26},{6,14,22..., dimensions={0}, use_global_device_ids=true | all-gather | bytes 983040 | tf_op jit(solution)/shard_map/all_gather | solution.py:112
  108.5 5.6 %collective-permute-start.2 = (bf16[128,3072]{1,0:T(8,128)(2,1)S(1)}, bf16[128,3072]{1,0:T(8,128)(2,1)}, u32[]{:S(2)}, u32[]{:S(2)}) collective-permute-start(bf16[128,3072]{1,0:T(8,128)(2,1)S(1)} %all_gather.10), channel_id=1, source_target_pairs={{0,4},{4,0},{8,12},{12,8},{16,20},{20,16},{24,28},{28,24},{1,5},{5... | collective-permute-start | bytes 2359304 | tf_op jit(solution)/shard_map/ppermute | solution.py:78
  114.1 0.8 multiply_bitcast_fusion.2
  114.9 1.2 collective-permute-done.2
  116.1 1.1 broadcast_select_fusion.2
  117.2 1.0 convolution_convert_fusion.5
  118.3 1.2 broadcast_select_fusion.4
  120.5 10.3 %collective-permute-start.4 = (bf16[192,640]{1,0:T(8,128)(2,1)S(1)}, bf16[192,640]{1,0:T(8,128)(2,1)S(1)}, u32[]{:S(2)}, u32[]{:S(2)}) collective-permute-start(bf16[192,640]{1,0:T(8,128)(2,1)S(1)} %pad_maximum_fusion.7), channel_id=1, source_target_pairs={{0,3},{1,2},{2,1},{3,0},{4,7},{5,6},{6,5},{7,4},{8,11},{9,10},{10,... | collective-permute-start | bytes 737288 | tf_op jit(solution)/shard_map/ppermute | solution.py:137
  130.9 5.2 %collective-permute-start.3 = (bf16[192,640]{1,0:T(8,128)(2,1)S(1)}, bf16[192,640]{1,0:T(8,128)(2,1)}, u32[]{:S(2)}, u32[]{:S(2)}) collective-permute-start(bf16[192,640]{1,0:T(8,128)(2,1)S(1)} %pad_maximum_fusion.6), channel_id=1, source_target_pairs={{0,1},{1,0},{2,3},{3,2},{4,5},{5,4},{6,7},{7,6},{8,9},{9,8},{10,11... | collective-permute-start | bytes 737288 | tf_op jit(solution)/shard_map/ppermute | solution.py:137
  136.1 1.1 copy.18
  137.2 3.6 %all-to-all-start.2 = ((bf16[4,256,512]{2,1,0:T(8,128)(2,1)}), bf16[4,256,512]{2,1,0:T(8,128)(2,1)S(1)}, u32[]{:S(2)}, u32[]{:S(2)}) async-start(bf16[4,256,512]{2,1,0:T(8,128)(2,1)} %bitcast.86), calls=%async_computation.2 | async-start | bytes 2097152 | tf_op jit(solution)/shard_map/all_to_all | solution.py:124
  140.9 1.7 convolution_convert_fusion.1
  142.6 13.1 %collective-permute-done.3 = bf16[192,640]{1,0:T(8,128)(2,1)} collective-permute-done((bf16[192,640]{1,0:T(8,128)(2,1)S(1)}, bf16[192,640]{1,0:T(8,128)(2,1)}, u32[]{:S(2)}, u32[]{:S(2)}) %collective-permute-start.3) | collective-permute-done | bytes 245792 | tf_op jit(solution)/shard_map/ppermute | solution.py:137
  155.7 0.8 fusion.8
  156.6 1.0 add_convert_fusion.2
  157.6 3.8 %all-to-all-start.4 = ((bf16[16,64,640]{2,1,0:T(8,128)(2,1)}), bf16[16,64,640]{2,1,0:T(8,128)(2,1)S(1)}, u32[]{:S(2)}, u32[]{:S(2)}) async-start(bf16[16,64,640]{2,1,0:T(8,128)(2,1)} %bitcast.37), calls=%async_computation.4 | async-start | bytes 2621440 | tf_op jit(solution)/shard_map/all_to_all | solution.py:124
  161.4 7.9 %collective-permute-start.6 = (bf16[160,640]{1,0:T(8,128)(2,1)S(1)}, bf16[160,640]{1,0:T(8,128)(2,1)S(1)}, u32[]{:S(2)}, u32[]{:S(2)}) collective-permute-start(bf16[160,640]{1,0:T(8,128)(2,1)S(1)} %pad_maximum_fusion.9), channel_id=1, source_target_pairs={{0,1},{1,0},{2,3},{3,2},{4,5},{5,4},{6,7},{7,6},{8,9},{9,8},{10,11... | collective-permute-start | bytes 614408 | tf_op jit(solution)/shard_map/ppermute | solution.py:137
  169.4 2.9 %collective-permute-start.5 = (bf16[160,640]{1,0:T(8,128)(2,1)S(1)}, bf16[160,640]{1,0:T(8,128)(2,1)S(1)}, u32[]{:S(2)}, u32[]{:S(2)}) collective-permute-start(bf16[160,640]{1,0:T(8,128)(2,1)S(1)} %pad_maximum_fusion.8), channel_id=1, source_target_pairs={{0,3},{1,2},{2,1},{3,0},{4,7},{5,6},{6,5},{7,4},{8,11},{9,10},{10,... | collective-permute-start | bytes 614408 | tf_op jit(solution)/shard_map/ppermute | solution.py:137
  172.3 3.2 %convolution_convert_fusion.2 = bf16[512,640]{1,0:T(8,128)(2,1)} fusion(bf16[1024,512]{1,0:T(8,128)(2,1)S(1)} %bitcast.91, bf16[1024,640]{1,0:T(8,128)(2,1)} %all-gather.2.cloned.1.call-done), kind=kOutput, calls=%fused_computation.4 | convolution fusion | flops 671416320 | bytes 3014656 | tf_op jit(solution)/shard_map/dot_general | solution.py:15
  175.5 8.5 %collective-permute-done.6 = bf16[160,640]{1,0:T(8,128)(2,1)S(1)} collective-permute-done((bf16[160,640]{1,0:T(8,128)(2,1)S(1)}, bf16[160,640]{1,0:T(8,128)(2,1)S(1)}, u32[]{:S(2)}, u32[]{:S(2)}) %collective-permute-start.6) | collective-permute-done | bytes 204832 | tf_op jit(solution)/shard_map/ppermute | solution.py:137
  184.1 1.8 collective-permute-done.5
  185.9 0.8 pad_maximum_fusion.5
  186.7 4.2 %all-to-all-start.3 = ((bf16[4,128,640]{2,1,0:T(8,128)(2,1)}), bf16[4,128,640]{2,1,0:T(8,128)(2,1)S(1)}, u32[]{:S(2)}, u32[]{:S(2)}) async-start(bf16[4,128,640]{2,1,0:T(8,128)(2,1)} %bitcast.34), calls=%async_computation.3 | async-start | bytes 1310720 | tf_op jit(solution)/shard_map/all_to_all | solution.py:124
  191.0 0.6 pad_maximum_fusion.10
  191.8 0.6 multiply_convert_fusion
  192.4 7.8 %all-to-all-done.3 = bf16[4,128,640]{2,1,0:T(8,128)(2,1)S(1)} async-done(((bf16[4,128,640]{2,1,0:T(8,128)(2,1)}), bf16[4,128,640]{2,1,0:T(8,128)(2,1)S(1)}, u32[]{:S(2)}, u32[]{:S(2)}) %all-to-all-start.3) | async-done | bytes 655392 | tf_op jit(solution)/shard_map/all_to_all | solution.py:124
  200.4 0.7 fusion.5
  (52 shorter events, 2.4 us)
Async XLA Ops:
  11.9 46.0 %all-to-all-start = ((bf16[16,128,640]{2,1,0:T(8,128)(2,1)}), bf16[16,128,640]{2,1,0:T(8,128)(2,1)S(1)}, u32[]{:S(2)}, u32[]{:S(2)}) async-start(bf16[16,128,640]{2,1,0:T(8,128)(2,1)} %broadcast_select_fusion), calls=%async_computation | async-start | bytes 5242880 | tf_op jit(solution)/shard_map/all_to_all | solution.py:92
  19.5 3.5 %copy-start.7 = (bf16[64,640]{1,0:T(8,128)(2,1)S(1)}, bf16[64,640]{1,0:T(8,128)(2,1)}, u32[]{:S(2)}) copy-start(bf16[64,640]{1,0:T(8,128)(2,1)} %param.15) | copy-start | bytes 245764
  47.5 0.7 copy-start.3
  50.2 6.7 %collective-permute-start = (bf16[128,1024]{1,0:T(8,128)(2,1)S(1)}, bf16[128,1024]{1,0:T(8,128)(2,1)}, u32[]{:S(2)}, u32[]{:S(2)}) collective-permute-start(bf16[128,1024]{1,0:T(8,128)(2,1)S(1)} %dynamic-slice_bitcast_fusion.1), channel_id=1, source_target_pairs={{0,4},{4,0},{8,12},{12,8},{16,20},{20,16},{24,28},{28,24},{1,5},{5... | collective-permute-start | bytes 786440 | tf_op jit(solution)/shard_map/ppermute | solution.py:78
  60.0 3.8 %collective-permute-start.1 = (bf16[128,2048]{1,0:T(8,128)(2,1)S(1)}, bf16[128,2048]{1,0:T(8,128)(2,1)S(1)}, u32[]{:S(2)}, u32[]{:S(2)}) collective-permute-start(bf16[128,2048]{1,0:T(8,128)(2,1)S(1)} %dynamic-slice_bitcast_fusion), channel_id=1, source_target_pairs={{0,4},{4,0},{8,12},{12,8},{16,20},{20,16},{24,28},{28,24},{1,5},{5... | collective-permute-start | bytes 1572872 | tf_op jit(solution)/shard_map/ppermute | solution.py:78
  64.9 27.2 %all-to-all-start.1 = ((bf16[4,32,3072]{2,1,0:T(8,128)(2,1)}), bf16[4,32,3072]{2,1,0:T(8,128)(2,1)S(1)}, u32[]{:S(2)}, u32[]{:S(2)}) async-start(bf16[4,32,3072]{2,1,0:T(8,128)(2,1)} %pad_maximum_fusion.1), calls=%async_computation.1 | async-start | bytes 1572864 | tf_op jit(solution)/shard_map/all_to_all | solution.py:108
  72.4 36.0 %all-gather.2.cloned.1.call-start = ((), (), s32[]{:S(2)}) async-start(), calls=%async_computation.5 | async-start | bytes 1638400 | tf_op jit(solution)/shard_map/all_gather | solution.py:96
  108.5 7.6 %collective-permute-start.2 = (bf16[128,3072]{1,0:T(8,128)(2,1)S(1)}, bf16[128,3072]{1,0:T(8,128)(2,1)}, u32[]{:S(2)}, u32[]{:S(2)}) collective-permute-start(bf16[128,3072]{1,0:T(8,128)(2,1)S(1)} %all_gather.10), channel_id=1, source_target_pairs={{0,4},{4,0},{8,12},{12,8},{16,20},{20,16},{24,28},{28,24},{1,5},{5... | collective-permute-start | bytes 2359304 | tf_op jit(solution)/shard_map/ppermute | solution.py:78
  118.2 2.2 %copy-start.1 = (bf16[256,640]{1,0:T(8,128)(2,1)}, bf16[256,640]{1,0:T(8,128)(2,1)S(1)}, u32[]{:S(2)}) copy-start(bf16[256,640]{1,0:T(8,128)(2,1)S(1)} %convolution_convert_fusion.5) | copy-start | bytes 983044
  118.2 1.5 copy-start
  119.5 0.9 copy-start.5
  120.5 36.1 %collective-permute-start.4 = (bf16[192,640]{1,0:T(8,128)(2,1)S(1)}, bf16[192,640]{1,0:T(8,128)(2,1)S(1)}, u32[]{:S(2)}, u32[]{:S(2)}) collective-permute-start(bf16[192,640]{1,0:T(8,128)(2,1)S(1)} %pad_maximum_fusion.7), channel_id=1, source_target_pairs={{0,3},{1,2},{2,1},{3,0},{4,7},{5,6},{6,5},{7,4},{8,11},{9,10},{10,... | collective-permute-start | bytes 737288 | tf_op jit(solution)/shard_map/ppermute | solution.py:137
  130.9 24.9 %collective-permute-start.3 = (bf16[192,640]{1,0:T(8,128)(2,1)S(1)}, bf16[192,640]{1,0:T(8,128)(2,1)}, u32[]{:S(2)}, u32[]{:S(2)}) collective-permute-start(bf16[192,640]{1,0:T(8,128)(2,1)S(1)} %pad_maximum_fusion.6), channel_id=1, source_target_pairs={{0,1},{1,0},{2,3},{3,2},{4,5},{5,4},{6,7},{7,6},{8,9},{9,8},{10,11... | collective-permute-start | bytes 737288 | tf_op jit(solution)/shard_map/ppermute | solution.py:137
  137.2 3.7 %copy-start.4 = (bf16[256,640]{1,0:T(8,128)(2,1)S(1)}, bf16[256,640]{1,0:T(8,128)(2,1)}, u32[]{:S(2)}) copy-start(bf16[256,640]{1,0:T(8,128)(2,1)} %copy-done.3) | copy-start | bytes 983044
  137.2 3.7 %copy-start.6 = (bf16[128,1024]{1,0:T(8,128)(2,1)S(1)}, bf16[128,1024]{1,0:T(8,128)(2,1)}, u32[]{:S(2)}) copy-start(bf16[128,1024]{1,0:T(8,128)(2,1)} %copy-done.5) | copy-start | bytes 786436
  137.2 20.4 %all-to-all-start.2 = ((bf16[4,256,512]{2,1,0:T(8,128)(2,1)}), bf16[4,256,512]{2,1,0:T(8,128)(2,1)S(1)}, u32[]{:S(2)}, u32[]{:S(2)}) async-start(bf16[4,256,512]{2,1,0:T(8,128)(2,1)} %bitcast.86), calls=%async_computation.2 | async-start | bytes 2097152 | tf_op jit(solution)/shard_map/all_to_all | solution.py:124
  140.9 15.7 %copy-start.2 = (bf16[256,640]{1,0:T(8,128)(2,1)S(1)}, bf16[256,640]{1,0:T(8,128)(2,1)}, u32[]{:S(2)}) copy-start(bf16[256,640]{1,0:T(8,128)(2,1)} %copy-done.1) | copy-start | bytes 983044
  157.6 29.1 %all-to-all-start.4 = ((bf16[16,64,640]{2,1,0:T(8,128)(2,1)}), bf16[16,64,640]{2,1,0:T(8,128)(2,1)S(1)}, u32[]{:S(2)}, u32[]{:S(2)}) async-start(bf16[16,64,640]{2,1,0:T(8,128)(2,1)} %bitcast.37), calls=%async_computation.4 | async-start | bytes 2621440 | tf_op jit(solution)/shard_map/all_to_all | solution.py:124
  161.4 22.6 %collective-permute-start.6 = (bf16[160,640]{1,0:T(8,128)(2,1)S(1)}, bf16[160,640]{1,0:T(8,128)(2,1)S(1)}, u32[]{:S(2)}, u32[]{:S(2)}) collective-permute-start(bf16[160,640]{1,0:T(8,128)(2,1)S(1)} %pad_maximum_fusion.9), channel_id=1, source_target_pairs={{0,1},{1,0},{2,3},{3,2},{4,5},{5,4},{6,7},{7,6},{8,9},{9,8},{10,11... | collective-permute-start | bytes 614408 | tf_op jit(solution)/shard_map/ppermute | solution.py:137
  169.4 16.5 %collective-permute-start.5 = (bf16[160,640]{1,0:T(8,128)(2,1)S(1)}, bf16[160,640]{1,0:T(8,128)(2,1)S(1)}, u32[]{:S(2)}, u32[]{:S(2)}) collective-permute-start(bf16[160,640]{1,0:T(8,128)(2,1)S(1)} %pad_maximum_fusion.8), channel_id=1, source_target_pairs={{0,3},{1,2},{2,1},{3,0},{4,7},{5,6},{6,5},{7,4},{8,11},{9,10},{10,... | collective-permute-start | bytes 614408 | tf_op jit(solution)/shard_map/ppermute | solution.py:137
  186.7 13.5 %all-to-all-start.3 = ((bf16[4,128,640]{2,1,0:T(8,128)(2,1)}), bf16[4,128,640]{2,1,0:T(8,128)(2,1)S(1)}, u32[]{:S(2)}, u32[]{:S(2)}) async-start(bf16[4,128,640]{2,1,0:T(8,128)(2,1)} %bitcast.34), calls=%async_computation.3 | async-start | bytes 1310720 | tf_op jit(solution)/shard_map/all_to_all | solution.py:124
Sparse Core Ops, SparseCore 0:
  75.3 30.5 all-gather.1

commit v2 on v1

--- a/solution.py
+++ b/solution.py
@@ -8,7 +8,6 @@
 BLOCK = 128
 BF = jnp.bfloat16
 F32 = jnp.float32
-CHIPS_Y = 4
 
 
 def dot(left, right, left_axis, right_axis):
@@ -67,12 +66,8 @@
     feat_blocks, unit_blocks = feats // BLOCK, units // BLOCK
     n_line = n_hid // 2
     c = h % 2
-    n_y = CHIPS_Y
-    n_x = n_tok // n_y
     pairs = [[2 * i + j for j in range(2)] for i in range(n_line)]
     lines = [[2 * i + j for i in range(n_line)] for j in range(2)]
-    along_y = [[n_x * i + j for i in range(n_y)] for j in range(n_x)]
-    along_x = [[n_x * i + j for j in range(n_x)] for i in range(n_y)]
 
     def hop_hid(value, distance):
         return lax.ppermute(value, "hid", [(i, i ^ distance) for i in range(n_hid)])
@@ -92,11 +87,6 @@
     weights = lax.all_to_all(spread, "tok", 0, 0).reshape(2 * units, feats)
     grad_rows = lax.all_gather(cotangent, "ffn", axis=0, tiled=True)
 
-    def gather_y(array):
-        return lax.all_gather(array, "tok", axis=0, tiled=True, axis_index_groups=along_y)
-
-    tokens_y = gather_y(tokens)
-
     def sum_cores(part):
         part = part.astype(BF).reshape(2, rows // 2, part.shape[1])
         half = pick(part, c).astype(F32) + hop_hid(pick(part, 1 - c), 1).astype(F32)
@@ -110,7 +100,6 @@
     )
     acts = activation(own, units, parts)
     mine = lax.all_gather(acts, "hid", axis=0, tiled=True, axis_index_groups=lines)
-    mine, tokens_y = lax.optimization_barrier((mine, tokens_y))
     other = hop_hid(mine, 1)
 
     def in_order(first, last):
@@ -120,11 +109,10 @@
     deltas = in_order(0, 2 * units)
     hidden = in_order(2 * units, 3 * units)
 
-    def exchange(parts, groups=None):
-        return lax.all_to_all(parts, "tok", 0, 0, axis_index_groups=groups)
-
-    quarter = deltas.reshape(rows, n_y, 2 * units // n_y).transpose(1, 0, 2)
-    quarter = exchange(quarter, along_y).reshape(n_y * rows, 2 * units // n_y)
+    delta_term = dot(deltas, tokens, 0, 0).astype(BF).reshape(n_tok, 2 * own, feats)
+    down_term = dot(hidden, grad_rows, 0, 0).astype(BF).reshape(n_tok, own, feats)
+    terms = lax.all_to_all(jnp.concatenate([delta_term, down_term], axis=1), "tok", 0, 0)
+    sums = total(terms) * (1.0 / n_tok)
 
     def beside(i):
         return i ^ 1
@@ -155,7 +143,6 @@
                 plus(pick(piece, second(f)), got[half + block :]),
             )
         )
-    waiting, quarter = lax.optimization_barrier((waiting, quarter))
     input_sums, mixed_sums = [], []
     for (first, second), (input_sum, own_sum, sent_sum) in zip(pairings, waiting):
         got = swap([input_sum, sent_sum], second)
@@ -164,13 +151,9 @@
     tokens_grad = jnp.concatenate(input_sums)
     mixed = jnp.concatenate(mixed_sums)
 
-    down_term = dot(hidden, grad_rows, 0, 0).astype(BF).reshape(n_tok, own, feats)
-    down_sum = total(exchange(down_term)) * (1.0 / n_tok)
-    delta_term = dot(quarter, tokens_y, 0, 0).astype(BF).reshape(n_x, 2 * own, feats)
-    sums = total(exchange(delta_term, along_x)) * (1.0 / n_tok)
     gate_grad = (sums[:own] * keep_gate.astype(F32)).astype(BF).T
-    up_grad = (sums[own:] * keep_up.astype(F32)).astype(BF).T
-    down_grad = (down_sum * keep_own_down.astype(F32)).astype(BF)
+    up_grad = (sums[own : 2 * own] * keep_up.astype(F32)).astype(BF).T
+    down_grad = (sums[2 * own :] * keep_own_down.astype(F32)).astype(BF)
     return (mixed, tokens_grad, gate_grad, up_grad, down_grad)
 
 

time: 210 us -> 186 us (0.89)
  blocking collectives: 39.9 us -> 66.7 us
  waiting for transfers between devices: 54.9 us -> 38.1 us
  starting transfers between devices: 66.5 us -> 50.9 us
  between operations: 14.5 us -> 1.06 us
  matrix products: 10.4 us -> 6.15 us
    all_to_all x0 -> x1, blocking collectives: none -> 26.9 us  [body(): lax.all_to_all(jnp.concatenate([both_half, grad_half], axis=2), 'hid', 0,...]
    all_to_all x4 -> x1, waiting for transfers between devices: 26.8 us -> 0.01 us  [body(): lax.all_to_all(jnp.concatenate([delta_term, down_term], axis=1), 'tok', 0...]
    all_to_all x4 -> x1, starting transfers between devices: 19.2 us -> 4.66 us  [body(): lax.all_to_all(jnp.concatenate([delta_term, down_term], axis=1), 'tok', 0...]
    ppermute x4, waiting for transfers between devices: 23.4 us -> 34.2 us  [swap(): return lax.ppermute(sent, 'ffn', [(i, pairing(i)) for i in range(n_ffn)])]
    dot_general x6, matrix products: 10.4 us -> 6.15 us  [dot(): lax.dot_general(left, right, (((left_axis,), (right_axis,)), ((), ())), p...]
    reduce_sum x2 -> x1, other arithmetic: 0.25 us -> 2.7 us  [total(): return jnp.sum(parts.astype(F32), axis=0)]
    concatenate x1, other arithmetic: 0.07 us -> 2.31 us  [body(): jnp.concatenate([delta_term, down_term], axis=1)]
    select_n x2, other arithmetic: 2.27 us -> 0.11 us  [in_order(): return jnp.concatenate([jnp.where(c == k, *halves) for k in range(2)])]
  transfers between devices with their start and end apart: 13 -> 9, of which waited for: 8 -> 7; matrix products, arithmetic and copies ran while one was open for 8% -> 6% of each run, Pallas kernels for 0% -> 0%
where the time goes in v2:
time: 186 us; the launch traced here: 185 us
  blocking collectives  66.7 us (36%)
  starting transfers between devices  50.9 us (27%)
  waiting for transfers between devices  38.1 us (20%)
  other arithmetic  17.5 us (9%)
  matrix products  6.15 us (3%)
  local copies, waits for them, and re-layouts  3.73 us (2%)
    ppermute x4, waiting for transfers between devices, swap(): return lax.ppermute(sent, 'ffn', [(i, pairing(i)) for i in range(n_ffn)])  34.2 us
    all_to_all x1, blocking collectives, body(): lax.all_to_all(jnp.concatenate([both_half, grad_half], axis=2), 'hid', 0,...  26.9 us
    ppermute x4, starting transfers between devices, swap(): return lax.ppermute(sent, 'ffn', [(i, pairing(i)) for i in range(n_ffn)])  25.1 us
    all_gather x1, blocking collectives, body(): grad_rows = lax.all_gather(cotangent, 'ffn', axis=0, tiled=True)  24.4 us
    all_gather x1, blocking collectives, body(): lax.all_gather(acts, 'hid', axis=0, tiled=True, axis_index_groups=lines)  15.3 us
    ppermute x3, starting transfers between devices, hop_hid(): return lax.ppermute(value, 'hid', [(i, i ^ distance) for i in range(n_hid)])  13.5 us
    all_to_all x1, starting transfers between devices, body(): weights = lax.all_to_all(spread, 'tok', 0, 0).reshape(2 * units, feats)  7.58 us
    dot_general x6, matrix products, dot(): lax.dot_general(left, right, (((left_axis,), (right_axis,)), ((), ())), p...  6.15 us
  transfers between devices with their start and end apart: 9, of which 7 were waited for; matrix products, arithmetic and copies ran while one was open for 6% of the time, Pallas kernels for 0%

profile of v2, /device:TPU:1, one launch (start us, length us, event | category | flops | bytes accessed | tf_op | source)
XLA Modules:
  0.0 185.0 jit_solution(15533332341639776895)
XLA Ops:
  0.7 0.1 iota.12
  0.8 0.8 convert_bitcast_fusion
  1.8 0.9 multiply_bitcast_fusion
  2.7 0.9 multiply_bitcast_fusion.1
  3.6 1.8 broadcast_select_fusion
  5.4 7.6 %all-to-all-start = ((bf16[16,128,640]{2,1,0:T(8,128)(2,1)}), bf16[16,128,640]{2,1,0:T(8,128)(2,1)S(1)}, u32[]{:S(2)}, u32[]{:S(2)}) async-start(bf16[16,128,640]{2,1,0:T(8,128)(2,1)} %broadcast_select_fusion), calls=%async_computation | async-start | bytes 5242880 | tf_op jit(solution)/shard_map/all_to_all | solution.py:87
  13.1 0.8 dynamic-slice_convert_fusion
  13.9 0.1 copy.13
  14.0 2.5 %bitcast_multiply_fusion = bf16[1024,640]{1,0:T(8,128)(2,1)} fusion(bf16[1024,640]{1,0:T(8,128)(2,1)} %param.11, bf16[8,640]{1,0:T(8,128)(2,1)S(1)} %broadcast_bitcast_fusion), kind=kLoop, calls=%fused_computation.6 | loop fusion | flops 655360 | bytes 2631680 | tf_op jit(solution)/shard_map/mul | solution.py:80
  16.6 24.4 %all_gather.6 = bf16[256,640]{1,0:T(8,128)(2,1)S(1)} all-gather(bf16[64,640]{1,0:T(8,128)(2,1)S(1)} %copy-done.7), channel_id=1, replica_groups=mesh['tok'=16,'hid'=8,'ffn'=4] {'ffn'}, dimensions={0}, use_global_device_ids=true | all-gather | bytes 409600 | tf_op jit(solution)/shard_map/all_gather | solution.py:88
  41.0 1.9 %convolution_convert_fusion.3 = bf16[1024,256]{0,1:T(8,128)(2,1)S(1)} fusion(bf16[1024,640]{1,0:T(8,128)(2,1)} %bitcast_multiply_fusion, bf16[256,640]{1,0:T(8,128)(2,1)S(1)} %all_gather.6), kind=kOutput, calls=%fused_computation.7 | convolution fusion | flops 335806464 | bytes 2162688 | tf_op jit(solution)/shard_map/dot_general | solution.py:14
  42.9 0.8 copy-done.4
  43.7 5.5 %collective-permute-start = (bf16[128,1024]{1,0:T(8,128)(2,1)S(1)}, bf16[128,1024]{1,0:T(8,128)(2,1)}, u32[]{:S(2)}, u32[]{:S(2)}) collective-permute-start(bf16[128,1024]{1,0:T(8,128)(2,1)S(1)} %dynamic-slice_bitcast_fusion.1), channel_id=1, source_target_pairs={{0,4},{4,0},{8,12},{12,8},{16,20},{20,16},{24,28},{28,24},{1,5},{5... | collective-permute-start | bytes 786440 | tf_op jit(solution)/shard_map/ppermute | solution.py:73
  49.2 1.3 collective-permute-done
  50.4 1.1 fusion.1
  51.6 1.0 convolution_convert_fusion.1
  52.6 0.5 copy-done.1
  53.2 2.3 %collective-permute-start.1 = (bf16[128,2048]{1,0:T(8,128)(2,1)S(1)}, bf16[128,2048]{1,0:T(8,128)(2,1)S(1)}, u32[]{:S(2)}, u32[]{:S(2)}) collective-permute-start(bf16[128,2048]{1,0:T(8,128)(2,1)S(1)} %dynamic-slice_bitcast_fusion), channel_id=1, source_target_pairs={{0,4},{4,0},{8,12},{12,8},{16,20},{20,16},{24,28},{28,24},{1,5},{5... | collective-permute-start | bytes 1572872 | tf_op jit(solution)/shard_map/ppermute | solution.py:73
  55.5 1.5 collective-permute-done.1
  57.0 0.1 fusion
  57.2 26.9 %all_to_all.15.refs_0_ = bf16[4,32,3072]{2,1,0:T(8,128)(2,1)S(1)} all-to-all(bf16[4,32,3072]{2,1,0:T(8,128)(2,1)S(1)} %pad_maximum_fusion.2), channel_id=1, replica_groups={{0,8,16,24},{4,12,20,28},{1,9,17,25},{5,13,21,29},{2,10,18,26},{6,14,22..., dimensions={0} | all-to-all | bytes 1572864 | tf_op jit(solution)/shard_map/all_to_all | solution.py:98
  84.1 0.9 shard_map.119
  85.0 15.3 %all_gather.7 = bf16[128,3072]{1,0:T(8,128)(2,1)S(1)} all-gather(bf16[32,3072]{1,0:T(8,128)(2,1)S(1)} %shard_map.119), channel_id=1, replica_groups={{0,8,16,24},{4,12,20,28},{1,9,17,25},{5,13,21,29},{2,10,18,26},{6,14,22..., dimensions={0}, use_global_device_ids=true | all-gather | bytes 983040 | tf_op jit(solution)/shard_map/all_gather | solution.py:102
  100.3 5.8 %collective-permute-start.2 = (bf16[128,3072]{1,0:T(8,128)(2,1)S(1)}, bf16[128,3072]{1,0:T(8,128)(2,1)S(1)}, u32[]{:S(2)}, u32[]{:S(2)}) collective-permute-start(bf16[128,3072]{1,0:T(8,128)(2,1)S(1)} %all_gather.7), channel_id=1, source_target_pairs={{0,4},{4,0},{8,12},{12,8},{16,20},{20,16},{24,28},{28,24},{1,5},{5... | collective-permute-start | bytes 2359304 | tf_op jit(solution)/shard_map/ppermute | solution.py:73
  106.2 0.8 bitcast_convert_fusion.2
  107.0 1.1 collective-permute-done.2
  108.1 0.7 copy-done.5
  108.8 0.6 convolution_convert_fusion.2
  109.4 0.1 broadcast_select_fusion.2
  109.5 1.0 convolution_convert_fusion
  110.5 2.3 %pad_maximum_fusion = bf16[16,192,640]{2,1,0:T(8,128)(2,1)} fusion(bf16[16,64,640]{2,1,0:T(8,128)(2,1)S(1)} %bitcast.83, bf16[16,128,640]{2,1,0:T(8,128)(2,1)S(1)} %bitcast.81), kind=kLoop, calls=%fused_computation.1 | loop fusion | flops 7864320 | bytes 7864320 | tf_op jit(solution)/shard_map/concatenate | solution.py:114
  112.8 4.7 %all-to-all-start.2 = ((bf16[16,192,640]{2,1,0:T(8,128)(2,1)}), bf16[16,192,640]{2,1,0:T(8,128)(2,1)}, u32[]{:S(2)}, u32[]{:S(2)}) async-start(bf16[16,192,640]{2,1,0:T(8,128)(2,1)} %pad_maximum_fusion), calls=%async_computation.2 | async-start | bytes 7864320 | tf_op jit(solution)/shard_map/all_to_all | solution.py:114
  117.5 0.6 convolution_convert_fusion.5
  118.2 1.1 copy-done.2
  119.3 1.0 convolution_convert_fusion.4
  120.4 9.8 %collective-permute-start.5 = (bf16[192,640]{1,0:T(8,128)(2,1)S(1)}, bf16[192,640]{1,0:T(8,128)(2,1)S(1)}, u32[]{:S(2)}, u32[]{:S(2)}) collective-permute-start(bf16[192,640]{1,0:T(8,128)(2,1)S(1)} %pad_maximum_fusion.10), channel_id=1, source_target_pairs={{0,3},{1,2},{2,1},{3,0},{4,7},{5,6},{6,5},{7,4},{8,11},{9,10},{10,... | collective-permute-start | bytes 737288 | tf_op jit(solution)/shard_map/ppermute | solution.py:125
  130.2 5.2 %collective-permute-start.3 = (bf16[192,640]{1,0:T(8,128)(2,1)S(1)}, bf16[192,640]{1,0:T(8,128)(2,1)S(1)}, u32[]{:S(2)}, u32[]{:S(2)}) collective-permute-start(bf16[192,640]{1,0:T(8,128)(2,1)S(1)} %pad_maximum_fusion.9), channel_id=1, source_target_pairs={{0,1},{1,0},{2,3},{3,2},{4,5},{5,4},{6,7},{7,6},{8,9},{9,8},{10,11... | collective-permute-start | bytes 737288 | tf_op jit(solution)/shard_map/ppermute | solution.py:125
  135.4 15.2 %collective-permute-done.5 = bf16[192,640]{1,0:T(8,128)(2,1)S(1)} collective-permute-done((bf16[192,640]{1,0:T(8,128)(2,1)S(1)}, bf16[192,640]{1,0:T(8,128)(2,1)S(1)}, u32[]{:S(2)}, u32[]{:S(2)}) %collective-permute-start.5) | collective-permute-done | bytes 245792 | tf_op jit(solution)/shard_map/ppermute | solution.py:125
  150.7 5.2 %collective-permute-done.3 = bf16[192,640]{1,0:T(8,128)(2,1)S(1)} collective-permute-done((bf16[192,640]{1,0:T(8,128)(2,1)S(1)}, bf16[192,640]{1,0:T(8,128)(2,1)S(1)}, u32[]{:S(2)}, u32[]{:S(2)}) %collective-permute-start.3) | collective-permute-done | bytes 245792 | tf_op jit(solution)/shard_map/ppermute | solution.py:125
  155.9 0.1 add_convert_fusion.3
  156.0 6.9 %collective-permute-start.6 = (bf16[160,640]{1,0:T(8,128)(2,1)S(1)}, bf16[160,640]{1,0:T(8,128)(2,1)S(1)}, u32[]{:S(2)}, u32[]{:S(2)}) collective-permute-start(bf16[160,640]{1,0:T(8,128)(2,1)S(1)} %pad_maximum_fusion.12), channel_id=1, source_target_pairs={{0,1},{1,0},{2,3},{3,2},{4,5},{5,4},{6,7},{7,6},{8,9},{9,8},{10,11... | collective-permute-start | bytes 614408 | tf_op jit(solution)/shard_map/ppermute | solution.py:125
  162.9 3.3 %collective-permute-start.4 = (bf16[160,640]{1,0:T(8,128)(2,1)S(1)}, bf16[160,640]{1,0:T(8,128)(2,1)S(1)}, u32[]{:S(2)}, u32[]{:S(2)}) collective-permute-start(bf16[160,640]{1,0:T(8,128)(2,1)S(1)} %pad_maximum_fusion.11), channel_id=1, source_target_pairs={{0,3},{1,2},{2,1},{3,0},{4,7},{5,6},{6,5},{7,4},{8,11},{9,10},{10,... | collective-permute-start | bytes 614408 | tf_op jit(solution)/shard_map/ppermute | solution.py:125
  166.2 6.2 %collective-permute-done.6 = bf16[160,640]{1,0:T(8,128)(2,1)S(1)} collective-permute-done((bf16[160,640]{1,0:T(8,128)(2,1)S(1)}, bf16[160,640]{1,0:T(8,128)(2,1)S(1)}, u32[]{:S(2)}, u32[]{:S(2)}) %collective-permute-start.6) | collective-permute-done | bytes 204832 | tf_op jit(solution)/shard_map/ppermute | solution.py:125
  172.4 7.7 %collective-permute-done.4 = bf16[160,640]{1,0:T(8,128)(2,1)S(1)} collective-permute-done((bf16[160,640]{1,0:T(8,128)(2,1)S(1)}, bf16[160,640]{1,0:T(8,128)(2,1)S(1)}, u32[]{:S(2)}, u32[]{:S(2)}) %collective-permute-start.4) | collective-permute-done | bytes 204832 | tf_op jit(solution)/shard_map/ppermute | solution.py:125
  180.1 0.6 pad_maximum_fusion.13
  180.8 0.8 pad_maximum_fusion.8
  181.6 2.7 %convert_reduce_fusion = f32[192,640]{1,0:T(8,128)S(1)} fusion(bf16[16,192,640]{2,1,0:T(8,128)(2,1)} %all-to-all-done.2), kind=kLoop, calls=%fused_computation | loop fusion | flops 3809280 | bytes 4423680 | tf_op jit(solution)/shard_map/reduce_sum | solution.py:20
  184.3 0.7 fusion.2
  (41 shorter events, 1.0 us)
Async XLA Ops:
  0.6 50.9 %copy-start = (bf16[256,640]{1,0:T(8,128)(2,1)S(1)}, bf16[256,640]{1,0:T(8,128)(2,1)}, u32[]{:S(2)}) copy-start(bf16[256,640]{1,0:T(8,128)(2,1)} %param.8) | copy-start | bytes 983044
  5.4 46.1 %all-to-all-start = ((bf16[16,128,640]{2,1,0:T(8,128)(2,1)}), bf16[16,128,640]{2,1,0:T(8,128)(2,1)S(1)}, u32[]{:S(2)}, u32[]{:S(2)}) async-start(bf16[16,128,640]{2,1,0:T(8,128)(2,1)} %broadcast_select_fusion), calls=%async_computation | async-start | bytes 5242880 | tf_op jit(solution)/shard_map/all_to_all | solution.py:87
  13.0 3.5 %copy-start.7 = (bf16[64,640]{1,0:T(8,128)(2,1)S(1)}, bf16[64,640]{1,0:T(8,128)(2,1)}, u32[]{:S(2)}) copy-start(bf16[64,640]{1,0:T(8,128)(2,1)} %param.15) | copy-start | bytes 245764
  42.9 0.8 copy-start.4
  43.7 6.7 %collective-permute-start = (bf16[128,1024]{1,0:T(8,128)(2,1)S(1)}, bf16[128,1024]{1,0:T(8,128)(2,1)}, u32[]{:S(2)}, u32[]{:S(2)}) collective-permute-start(bf16[128,1024]{1,0:T(8,128)(2,1)S(1)} %dynamic-slice_bitcast_fusion.1), channel_id=1, source_target_pairs={{0,4},{4,0},{8,12},{12,8},{16,20},{20,16},{24,28},{28,24},{1,5},{5... | collective-permute-start | bytes 786440 | tf_op jit(solution)/shard_map/ppermute | solution.py:73
  51.6 1.6 copy-start.1
  53.2 3.8 %collective-permute-start.1 = (bf16[128,2048]{1,0:T(8,128)(2,1)S(1)}, bf16[128,2048]{1,0:T(8,128)(2,1)S(1)}, u32[]{:S(2)}, u32[]{:S(2)}) collective-permute-start(bf16[128,2048]{1,0:T(8,128)(2,1)S(1)} %dynamic-slice_bitcast_fusion), channel_id=1, source_target_pairs={{0,4},{4,0},{8,12},{12,8},{16,20},{20,16},{24,28},{28,24},{1,5},{5... | collective-permute-start | bytes 1572872 | tf_op jit(solution)/shard_map/ppermute | solution.py:73
  100.3 7.7 %collective-permute-start.2 = (bf16[128,3072]{1,0:T(8,128)(2,1)S(1)}, bf16[128,3072]{1,0:T(8,128)(2,1)S(1)}, u32[]{:S(2)}, u32[]{:S(2)}) collective-permute-start(bf16[128,3072]{1,0:T(8,128)(2,1)S(1)} %all_gather.7), channel_id=1, source_target_pairs={{0,4},{4,0},{8,12},{12,8},{16,20},{20,16},{24,28},{28,24},{1,5},{5... | collective-permute-start | bytes 2359304 | tf_op jit(solution)/shard_map/ppermute | solution.py:73
  108.1 0.7 copy-start.5
  112.8 4.7 %copy-start.3 = (bf16[1024,640]{1,0:T(8,128)(2,1)S(1)}, bf16[1024,640]{1,0:T(8,128)(2,1)}, u32[]{:S(2)}) copy-start(bf16[1024,640]{1,0:T(8,128)(2,1)} %bitcast_multiply_fusion) | copy-start | bytes 3932164
  112.8 4.7 %copy-start.6 = (bf16[128,1024]{1,0:T(8,128)(2,1)S(1)}, bf16[128,1024]{1,0:T(8,128)(2,1)}, u32[]{:S(2)}) copy-start(bf16[128,1024]{1,0:T(8,128)(2,1)} %copy-done.5) | copy-start | bytes 786436
  112.8 68.8 %all-to-all-start.2 = ((bf16[16,192,640]{2,1,0:T(8,128)(2,1)}), bf16[16,192,640]{2,1,0:T(8,128)(2,1)}, u32[]{:S(2)}, u32[]{:S(2)}) async-start(bf16[16,192,640]{2,1,0:T(8,128)(2,1)} %pad_maximum_fusion), calls=%async_computation.2 | async-start | bytes 7864320 | tf_op jit(solution)/shard_map/all_to_all | solution.py:114
  117.5 1.7 copy-start.2
  120.4 30.3 %collective-permute-start.5 = (bf16[192,640]{1,0:T(8,128)(2,1)S(1)}, bf16[192,640]{1,0:T(8,128)(2,1)S(1)}, u32[]{:S(2)}, u32[]{:S(2)}) collective-permute-start(bf16[192,640]{1,0:T(8,128)(2,1)S(1)} %pad_maximum_fusion.10), channel_id=1, source_target_pairs={{0,3},{1,2},{2,1},{3,0},{4,7},{5,6},{6,5},{7,4},{8,11},{9,10},{10,... | collective-permute-start | bytes 737288 | tf_op jit(solution)/shard_map/ppermute | solution.py:125
  130.2 25.7 %collective-permute-start.3 = (bf16[192,640]{1,0:T(8,128)(2,1)S(1)}, bf16[192,640]{1,0:T(8,128)(2,1)S(1)}, u32[]{:S(2)}, u32[]{:S(2)}) collective-permute-start(bf16[192,640]{1,0:T(8,128)(2,1)S(1)} %pad_maximum_fusion.9), channel_id=1, source_target_pairs={{0,1},{1,0},{2,3},{3,2},{4,5},{5,4},{6,7},{7,6},{8,9},{9,8},{10,11... | collective-permute-start | bytes 737288 | tf_op jit(solution)/shard_map/ppermute | solution.py:125
  156.0 16.4 %collective-permute-start.6 = (bf16[160,640]{1,0:T(8,128)(2,1)S(1)}, bf16[160,640]{1,0:T(8,128)(2,1)S(1)}, u32[]{:S(2)}, u32[]{:S(2)}) collective-permute-start(bf16[160,640]{1,0:T(8,128)(2,1)S(1)} %pad_maximum_fusion.12), channel_id=1, source_target_pairs={{0,1},{1,0},{2,3},{3,2},{4,5},{5,4},{6,7},{7,6},{8,9},{9,8},{10,11... | collective-permute-start | bytes 614408 | tf_op jit(solution)/shard_map/ppermute | solution.py:125
  162.9 17.2 %collective-permute-start.4 = (bf16[160,640]{1,0:T(8,128)(2,1)S(1)}, bf16[160,640]{1,0:T(8,128)(2,1)S(1)}, u32[]{:S(2)}, u32[]{:S(2)}) collective-permute-start(bf16[160,640]{1,0:T(8,128)(2,1)S(1)} %pad_maximum_fusion.11), channel_id=1, source_target_pairs={{0,3},{1,2},{2,1},{3,0},{4,7},{5,6},{6,5},{7,4},{8,11},{9,10},{10,... | collective-permute-start | bytes 614408 | tf_op jit(solution)/shard_map/ppermute | solution.py:125

commit v3 on v2

--- a/solution.py
+++ b/solution.py
@@ -81,10 +81,19 @@
         units, feats
     )
 
-    is_gate = lax.broadcasted_iota(jnp.int32, (n_tok, 2, own, feats), 1) == 0
-    spread = jnp.where(is_gate, (gate_weight.T * keep_gate)[None, None], (up_weight.T * keep_up)[None, None])
-    spread = spread.reshape(n_tok, 2 * own, feats)
-    weights = lax.all_to_all(spread, "tok", 0, 0).reshape(2 * units, feats)
+    spread = jnp.broadcast_to(
+        jnp.concatenate([gate_weight.T, up_weight.T])[None], (n_tok, 2 * own, feats)
+    )
+    gathered = lax.all_to_all(spread, "tok", 0, 0)
+    first_block = f * unit_blocks
+    keep_both = jnp.stack(
+        [
+            keep_rows(mask.T, first_block, unit_blocks, h * feat_blocks, feat_blocks)
+            for mask in (gate_mask, up_mask)
+        ],
+        axis=1,
+    )
+    keep_both = jnp.repeat(keep_both, n_tok // unit_blocks, axis=0)
     grad_rows = lax.all_gather(cotangent, "ffn", axis=0, tiled=True)
 
     def sum_cores(part):
@@ -93,7 +102,9 @@
         return half.astype(BF).reshape(n_line, rows // n_hid, part.shape[2])
 
     grad_half = sum_cores(dot(grad_rows, down_eff, 1, 1))
-    weights, grad_half = lax.optimization_barrier((weights, grad_half))
+    gathered, grad_half = lax.optimization_barrier((gathered, grad_half))
+    weights = gathered.reshape(n_tok, 2, own, feats) * keep_both[:, :, None, :]
+    weights = weights.reshape(2 * units, feats)
     both_half = sum_cores(dot(tokens, weights, 1, 1))
     parts = lax.all_to_all(
         jnp.concatenate([both_half, grad_half], axis=2), "hid", 0, 0, axis_index_groups=lines
@@ -120,36 +131,29 @@
     def around(i):
         return n_ffn - 1 - i
 
-    def swap(values, pairing):
-        sent = jnp.concatenate(values)
-        return lax.ppermute(sent, "ffn", [(i, pairing(i)) for i in range(n_ffn)])
+    def swap(values, by_core):
+        perm = [
+            (j * n_ffn + i, j * n_ffn + by_core[j % 2](i)) for j in range(n_hid) for i in range(n_ffn)
+        ]
+        return lax.ppermute(jnp.concatenate(values), ("hid", "ffn"), perm)
 
     def plus(left, right):
         return (left.astype(F32) + right.astype(F32)).astype(BF)
 
-    input_part = dot(deltas, weights, 1, 0).astype(BF).reshape(2, rows // 2, feats)
-    mixed_part = dot(hidden, down_eff, 1, 0).astype(BF)
-    mixed_part = mixed_part.reshape(n_ffn, 2, rows // n_ffn // 2, feats)
-    half, block = rows // 2, rows // n_ffn // 2
-    pairings = ((beside, around), (around, beside))
-    waiting = []
-    for k, (first, second) in enumerate(pairings):
-        piece = mixed_part[:, k]
-        got = swap([input_part[k], pick(piece, first(f)), pick(piece, second(first(f)))], first)
-        waiting.append(
-            (
-                plus(input_part[k], got[:half]),
-                plus(pick(piece, f), got[half : half + block]),
-                plus(pick(piece, second(f)), got[half + block :]),
-            )
-        )
-    input_sums, mixed_sums = [], []
-    for (first, second), (input_sum, own_sum, sent_sum) in zip(pairings, waiting):
-        got = swap([input_sum, sent_sum], second)
-        input_sums.append(plus(input_sum, got[:half]))
-        mixed_sums.append(plus(own_sum, got[half:]))
-    tokens_grad = jnp.concatenate(input_sums)
-    mixed = jnp.concatenate(mixed_sums)
+    first = jnp.where(c == 0, beside(f), around(f))
+    second = jnp.where(c == 0, around(f), beside(f))
+    across = n_ffn - 1 - beside(f)
+    block = rows // n_ffn
+    input_part = dot(deltas, weights, 1, 0).astype(BF)
+    mixed_part = dot(hidden, down_eff, 1, 0).astype(BF).reshape(n_ffn, block, feats)
+    got = swap([input_part, pick(mixed_part, first), pick(mixed_part, across)], (beside, around))
+    input_sum = plus(input_part, got[:rows])
+    own_sum = plus(pick(mixed_part, f), got[rows : rows + block])
+    sent_sum = plus(pick(mixed_part, second), got[rows + block :])
+    got = swap([input_sum, sent_sum], (around, beside))
+    got, sums = lax.optimization_barrier((got, sums))
+    tokens_grad = plus(input_sum, got[:rows])
+    mixed = plus(own_sum, got[rows:])
 
     gate_grad = (sums[:own] * keep_gate.astype(F32)).astype(BF).T
     up_grad = (sums[own : 2 * own] * keep_up.astype(F32)).astype(BF).T

time: 186 us -> 182 us (0.978)
  starting transfers between devices: 50.9 us -> 42.7 us
  matrix products: 6.15 us -> 8.64 us
  local copies, waits for them, and re-layouts: 3.73 us -> 6.08 us
    ppermute x4 -> x2, waiting for transfers between devices: 34.2 us -> 19.3 us  [swap(): return lax.ppermute(jnp.concatenate(values), ('hid', 'ffn'), perm)]
    all_to_all x1, waiting for transfers between devices: 0.01 us -> 15 us  [body(): lax.all_to_all(jnp.concatenate([delta_term, down_term], axis=1), 'tok', 0...]
    ppermute x4 -> x2, starting transfers between devices: 25.1 us -> 17.3 us  [swap(): return lax.ppermute(jnp.concatenate(values), ('hid', 'ffn'), perm)]
    convert_element_type x7 -> x4, other arithmetic: 0.24 us -> 3.35 us  [plus(): return (left.astype(F32) + right.astype(F32)).astype(BF)]
    broadcast_in_dim x2, local copies, waits for them, and re-layouts: 0.03 us -> 2.56 us  [the longest x1 1.81 us: body(): jnp.broadcast_to(jnp.concatenate([gate_weight.T, up_weight.T])[None], (n_...]
    dot_general x6, matrix products: 6.15 us -> 8.64 us  [dot(): lax.dot_general(left, right, (((left_axis,), (right_axis,)), ((), ())), p...]
  transfers between devices with their start and end apart: 9 -> 7, of which waited for: 7 -> 4; matrix products, arithmetic and copies ran while one was open for 6% -> 10% of each run, Pallas kernels for 0% -> 0%
where the time goes in v3:
time: 182 us; the launch traced here: 181 us
  blocking collectives  66.2 us (36%)
  starting transfers between devices  42.7 us (23%)
  waiting for transfers between devices  38 us (21%)
  other arithmetic  17.9 us (10%)
  matrix products  8.64 us (5%)
  local copies, waits for them, and re-layouts  6.08 us (3%)
    all_to_all x1, blocking collectives, body(): lax.all_to_all(jnp.concatenate([both_half, grad_half], axis=2), 'hid', 0,...  26.4 us
    all_gather x1, blocking collectives, body(): grad_rows = lax.all_gather(cotangent, 'ffn', axis=0, tiled=True)  24.4 us
    ppermute x2, waiting for transfers between devices, swap(): return lax.ppermute(jnp.concatenate(values), ('hid', 'ffn'), perm)  19.3 us
    ppermute x2, starting transfers between devices, swap(): return lax.ppermute(jnp.concatenate(values), ('hid', 'ffn'), perm)  17.3 us
    all_gather x1, blocking collectives, body(): lax.all_gather(acts, 'hid', axis=0, tiled=True, axis_index_groups=lines)  15.3 us
    all_to_all x1, waiting for transfers between devices, body(): lax.all_to_all(jnp.concatenate([delta_term, down_term], axis=1), 'tok', 0...  15 us
    ppermute x3, starting transfers between devices, hop_hid(): return lax.ppermute(value, 'hid', [(i, i ^ distance) for i in range(n_hid)])  13.2 us
    dot_general x6, matrix products, dot(): lax.dot_general(left, right, (((left_axis,), (right_axis,)), ((), ())), p...  8.64 us
  transfers between devices with their start and end apart: 7, of which 4 were waited for; matrix products, arithmetic and copies ran while one was open for 10% of the time, Pallas kernels for 0%

profile of v3, /device:TPU:1, one launch (start us, length us, event | category | flops | bytes accessed | tf_op | source)
XLA Modules:
  0.0 181.4 jit_solution(17256319313252794138)
XLA Ops:
  0.6 1.0 pad_maximum_fusion.10
  1.6 1.8 broadcast_in_dim.27
  3.4 7.6 %all-to-all-start = ((bf16[16,128,640]{2,1,0:T(8,128)(2,1)}), bf16[16,128,640]{2,1,0:T(8,128)(2,1)S(1)}, u32[]{:S(2)}, u32[]{:S(2)}) async-start(bf16[16,128,640]{2,1,0:T(8,128)(2,1)} %broadcast_in_dim.27), calls=%async_computation | async-start | bytes 5242880 | tf_op jit(solution)/shard_map/all_to_all | solution.py:87
  11.1 0.8 dynamic-slice_convert_fusion.2
  11.9 0.1 copy.14
  12.0 0.1 broadcast_bitcast_fusion.2
  12.0 2.5 %bitcast_multiply_fusion.1 = bf16[1024,640]{1,0:T(8,128)(2,1)} fusion(bf16[1024,640]{1,0:T(8,128)(2,1)} %param.11, bf16[8,640]{1,0:T(8,128)(2,1)S(1)} %broadcast_bitcast_fusion.2), kind=kLoop, calls=%fused_computation.6 | loop fusion | flops 655360 | bytes 2631680 | tf_op jit(solution)/shard_map/mul | solution.py:80
  14.5 24.4 %all_gather.6 = bf16[256,640]{1,0:T(8,128)(2,1)S(1)} all-gather(bf16[64,640]{1,0:T(8,128)(2,1)S(1)} %copy-done.9), channel_id=1, replica_groups=mesh['tok'=16,'hid'=8,'ffn'=4] {'ffn'}, dimensions={0}, use_global_device_ids=true | all-gather | bytes 409600 | tf_op jit(solution)/shard_map/all_gather | solution.py:97
  39.0 1.9 %convolution_convert_fusion.3 = bf16[1024,256]{0,1:T(8,128)(2,1)S(1)} fusion(bf16[1024,640]{1,0:T(8,128)(2,1)} %bitcast_multiply_fusion.1, bf16[256,640]{1,0:T(8,128)(2,1)S(1)} %all_gather.6), kind=kOutput, calls=%fused_computation.7 | convolution fusion | flops 335806464 | bytes 2162688 | tf_op jit(solution)/shard_map/dot_general | solution.py:14
  40.9 0.8 copy-done.3
  41.7 5.5 %collective-permute-start = (bf16[128,1024]{1,0:T(8,128)(2,1)S(1)}, bf16[128,1024]{1,0:T(8,128)(2,1)}, u32[]{:S(2)}, u32[]{:S(2)}) collective-permute-start(bf16[128,1024]{1,0:T(8,128)(2,1)S(1)} %dynamic-slice_bitcast_fusion.1), channel_id=1, source_target_pairs={{0,4},{4,0},{8,12},{12,8},{16,20},{20,16},{24,28},{28,24},{1,5},{5... | collective-permute-start | bytes 786440 | tf_op jit(solution)/shard_map/ppermute | solution.py:73
  47.2 0.8 fusion.6
  48.0 0.1 copy.16
  48.1 0.1 copy.15
  48.3 0.6 copy.17
  49.0 1.1 fusion.1
  50.1 0.8 broadcast_in_dim.31
  50.8 0.5 bitcast_multiply_fusion
  51.3 1.0 convolution_convert_fusion.1
  52.4 0.6 copy-done.1
  53.0 1.9 %collective-permute-start.1 = (bf16[128,2048]{1,0:T(8,128)(2,1)S(1)}, bf16[128,2048]{1,0:T(8,128)(2,1)S(1)}, u32[]{:S(2)}, u32[]{:S(2)}) collective-permute-start(bf16[128,2048]{1,0:T(8,128)(2,1)S(1)} %dynamic-slice_bitcast_fusion), channel_id=1, source_target_pairs={{0,4},{4,0},{8,12},{12,8},{16,20},{20,16},{24,28},{28,24},{1,5},{5... | collective-permute-start | bytes 1572872 | tf_op jit(solution)/shard_map/ppermute | solution.py:73
  54.9 1.9 %collective-permute-done.1 = bf16[128,2048]{1,0:T(8,128)(2,1)S(1)} collective-permute-done((bf16[128,2048]{1,0:T(8,128)(2,1)S(1)}, bf16[128,2048]{1,0:T(8,128)(2,1)S(1)}, u32[]{:S(2)}, u32[]{:S(2)}) %collective-permute-start.1) | collective-permute-done | bytes 524320 | tf_op jit(solution)/shard_map/ppermute | solution.py:73
  56.8 0.1 fusion
  57.0 26.4 %all_to_all.15.refs_0_ = bf16[4,32,3072]{2,1,0:T(8,128)(2,1)S(1)} all-to-all(bf16[4,32,3072]{2,1,0:T(8,128)(2,1)S(1)} %pad_maximum_fusion.2), channel_id=1, replica_groups={{0,8,16,24},{4,12,20,28},{1,9,17,25},{5,13,21,29},{2,10,18,26},{6,14,22..., dimensions={0} | all-to-all | bytes 1572864 | tf_op jit(solution)/shard_map/all_to_all | solution.py:109
  83.4 0.9 shard_map.119
  84.3 15.3 %all_gather.7 = bf16[128,3072]{1,0:T(8,128)(2,1)S(1)} all-gather(bf16[32,3072]{1,0:T(8,128)(2,1)S(1)} %shard_map.119), channel_id=1, replica_groups={{0,8,16,24},{4,12,20,28},{1,9,17,25},{5,13,21,29},{2,10,18,26},{6,14,22..., dimensions={0}, use_global_device_ids=true | all-gather | bytes 983040 | tf_op jit(solution)/shard_map/all_gather | solution.py:113
  99.6 5.8 %collective-permute-start.2 = (bf16[128,3072]{1,0:T(8,128)(2,1)S(1)}, bf16[128,3072]{1,0:T(8,128)(2,1)S(1)}, u32[]{:S(2)}, u32[]{:S(2)}) collective-permute-start(bf16[128,3072]{1,0:T(8,128)(2,1)S(1)} %all_gather.7), channel_id=1, source_target_pairs={{0,4},{4,0},{8,12},{12,8},{16,20},{20,16},{24,28},{28,24},{1,5},{5... | collective-permute-start | bytes 2359304 | tf_op jit(solution)/shard_map/ppermute | solution.py:73
  105.4 1.9 %collective-permute-done.2 = bf16[128,3072]{1,0:T(8,128)(2,1)S(1)} collective-permute-done((bf16[128,3072]{1,0:T(8,128)(2,1)S(1)}, bf16[128,3072]{1,0:T(8,128)(2,1)S(1)}, u32[]{:S(2)}, u32[]{:S(2)}) %collective-permute-start.2) | collective-permute-done | bytes 786464 | tf_op jit(solution)/shard_map/ppermute | solution.py:73
  107.4 0.6 convolution_convert_fusion.2
  108.0 0.1 broadcast_select_fusion.1
  108.1 1.0 convolution_convert_fusion
  109.2 2.3 %pad_maximum_fusion = bf16[16,192,640]{2,1,0:T(8,128)(2,1)} fusion(bf16[16,64,640]{2,1,0:T(8,128)(2,1)S(1)} %bitcast.79, bf16[16,128,640]{2,1,0:T(8,128)(2,1)S(1)} %bitcast.77), kind=kLoop, calls=%fused_computation.1 | loop fusion | flops 7864320 | bytes 7864320 | tf_op jit(solution)/shard_map/concatenate | solution.py:125
  111.5 4.7 %all-to-all-start.2 = ((bf16[16,192,640]{2,1,0:T(8,128)(2,1)}), bf16[16,192,640]{2,1,0:T(8,128)(2,1)}, u32[]{:S(2)}, u32[]{:S(2)}) async-start(bf16[16,192,640]{2,1,0:T(8,128)(2,1)} %pad_maximum_fusion), calls=%async_computation.2 | async-start | bytes 7864320 | tf_op jit(solution)/shard_map/all_to_all | solution.py:125
  116.2 0.9 bitcast_convert_fusion
  117.2 1.9 %convolution_convert_fusion.5 = bf16[256,640]{1,0:T(8,128)(2,1)S(1)} fusion(bf16[1024,640]{1,0:T(8,128)(2,1)} %bitcast_multiply_fusion.1, bf16[128,1024]{1,0:T(8,128)(2,1)S(1)} %copy-done.8, bf16[128,1024]{1,0:T(8,128)(2,1)S(1)} %get-tuple-element.15), kind=kOutput, calls=%fused_computation.9 | convolution fusion | flops 336756736 | bytes 2162688 | tf_op jit(solution)/shard_map/dot_general | solution.py:14
  119.1 0.7 copy-done.6
  119.8 2.2 %convolution_convert_fusion.4 = bf16[256,640]{1,0:T(8,128)(2,1)S(1)} fusion(bf16[2048,640]{1,0:T(8,128)(2,1)S(1)} %copy-done.2, bf16[128,2048]{1,0:T(8,128)(2,1)} %copy-done.5, bf16[128,2048]{1,0:T(8,128)(2,1)} %copy-done.4), kind=kOutput, calls=%fused_computation.8 | convolution fusion | flops 673349632 | bytes 3997696 | tf_op jit(solution)/shard_map/dot_general | solution.py:14
  122.0 9.8 %collective-permute-start.3 = (bf16[384,640]{1,0:T(8,128)(2,1)S(1)}, bf16[384,640]{1,0:T(8,128)(2,1)S(1)}, u32[]{:S(2)}, u32[]{:S(2)}) collective-permute-start(bf16[384,640]{1,0:T(8,128)(2,1)S(1)} %pad_maximum_fusion.6), channel_id=1, source_target_pairs={{0,1},{1,0},{2,3},{3,2},{4,7},{5,6},{6,5},{7,4},{8,9},{9,8},{10,11... | collective-permute-start | bytes 1474568 | tf_op jit(solution)/shard_map/ppermute | solution.py:138
  131.8 0.8 bitcast_convert_fusion.1
  132.7 19.3 %collective-permute-done.3 = bf16[384,640]{1,0:T(8,128)(2,1)S(1)} collective-permute-done((bf16[384,640]{1,0:T(8,128)(2,1)S(1)}, bf16[384,640]{1,0:T(8,128)(2,1)S(1)}, u32[]{:S(2)}, u32[]{:S(2)}) %collective-permute-start.3) | collective-permute-done | bytes 491552 | tf_op jit(solution)/shard_map/ppermute | solution.py:138
  152.0 0.9 fusion.2
  152.9 0.1 add_convert_fusion.1
  153.1 7.6 %collective-permute-start.4 = (bf16[320,640]{1,0:T(8,128)(2,1)S(1)}, bf16[320,640]{1,0:T(8,128)(2,1)S(1)}, u32[]{:S(2)}, u32[]{:S(2)}) collective-permute-start(bf16[320,640]{1,0:T(8,128)(2,1)S(1)} %pad_maximum_fusion.7), channel_id=1, source_target_pairs={{0,3},{1,2},{2,1},{3,0},{4,5},{5,4},{6,7},{7,6},{8,11},{9,10},{10,... | collective-permute-start | bytes 1228808 | tf_op jit(solution)/shard_map/ppermute | solution.py:138
  160.6 15.0 %all-to-all-done.2 = bf16[16,192,640]{2,1,0:T(8,128)(2,1)} async-done(((bf16[16,192,640]{2,1,0:T(8,128)(2,1)}), bf16[16,192,640]{2,1,0:T(8,128)(2,1)}, u32[]{:S(2)}, u32[]{:S(2)}) %all-to-all-start.2) | async-done | bytes 3932192 | tf_op jit(solution)/shard_map/all_to_all | solution.py:125
  175.6 2.7 %convert_reduce_fusion = f32[192,640]{1,0:T(8,128)S(1)} fusion(bf16[16,192,640]{2,1,0:T(8,128)(2,1)} %all-to-all-done.2), kind=kLoop, calls=%fused_computation | loop fusion | flops 3809280 | bytes 4423680 | tf_op jit(solution)/shard_map/reduce_sum | solution.py:20
  178.4 0.8 add_convert_fusion
  179.2 0.7 multiply_convert_fusion
  179.9 1.6 add_convert_fusion.2
  (34 shorter events, 0.7 us)
Async XLA Ops:
  0.6 50.7 %copy-start = (bf16[256,640]{1,0:T(8,128)(2,1)S(1)}, bf16[256,640]{1,0:T(8,128)(2,1)}, u32[]{:S(2)}) copy-start(bf16[256,640]{1,0:T(8,128)(2,1)} %param.8) | copy-start | bytes 983044
  3.4 46.6 %all-to-all-start = ((bf16[16,128,640]{2,1,0:T(8,128)(2,1)}), bf16[16,128,640]{2,1,0:T(8,128)(2,1)S(1)}, u32[]{:S(2)}, u32[]{:S(2)}) async-start(bf16[16,128,640]{2,1,0:T(8,128)(2,1)} %broadcast_in_dim.27), calls=%async_computation | async-start | bytes 5242880 | tf_op jit(solution)/shard_map/all_to_all | solution.py:87
  11.0 3.5 %copy-start.9 = (bf16[64,640]{1,0:T(8,128)(2,1)S(1)}, bf16[64,640]{1,0:T(8,128)(2,1)}, u32[]{:S(2)}) copy-start(bf16[64,640]{1,0:T(8,128)(2,1)} %param.15) | copy-start | bytes 245764
  40.9 0.8 copy-start.3
  41.7 7.2 %collective-permute-start = (bf16[128,1024]{1,0:T(8,128)(2,1)S(1)}, bf16[128,1024]{1,0:T(8,128)(2,1)}, u32[]{:S(2)}, u32[]{:S(2)}) collective-permute-start(bf16[128,1024]{1,0:T(8,128)(2,1)S(1)} %dynamic-slice_bitcast_fusion.1), channel_id=1, source_target_pairs={{0,4},{4,0},{8,12},{12,8},{16,20},{20,16},{24,28},{28,24},{1,5},{5... | collective-permute-start | bytes 786440 | tf_op jit(solution)/shard_map/ppermute | solution.py:73
  51.3 1.6 copy-start.1
  53.0 3.8 %collective-permute-start.1 = (bf16[128,2048]{1,0:T(8,128)(2,1)S(1)}, bf16[128,2048]{1,0:T(8,128)(2,1)S(1)}, u32[]{:S(2)}, u32[]{:S(2)}) collective-permute-start(bf16[128,2048]{1,0:T(8,128)(2,1)S(1)} %dynamic-slice_bitcast_fusion), channel_id=1, source_target_pairs={{0,4},{4,0},{8,12},{12,8},{16,20},{20,16},{24,28},{28,24},{1,5},{5... | collective-permute-start | bytes 1572872 | tf_op jit(solution)/shard_map/ppermute | solution.py:73
  99.6 7.7 %collective-permute-start.2 = (bf16[128,3072]{1,0:T(8,128)(2,1)S(1)}, bf16[128,3072]{1,0:T(8,128)(2,1)S(1)}, u32[]{:S(2)}, u32[]{:S(2)}) collective-permute-start(bf16[128,3072]{1,0:T(8,128)(2,1)S(1)} %all_gather.7), channel_id=1, source_target_pairs={{0,4},{4,0},{8,12},{12,8},{16,20},{20,16},{24,28},{28,24},{1,5},{5... | collective-permute-start | bytes 2359304 | tf_op jit(solution)/shard_map/ppermute | solution.py:73
  107.4 1.8 copy-start.7
  108.1 1.1 copy-start.4
  108.1 1.1 copy-start.5
  111.5 5.7 %copy-start.8 = (bf16[128,1024]{1,0:T(8,128)(2,1)S(1)}, bf16[128,1024]{1,0:T(8,128)(2,1)}, u32[]{:S(2)}) copy-start(bf16[128,1024]{1,0:T(8,128)(2,1)} %copy-done.7) | copy-start | bytes 786436
  111.5 64.1 %all-to-all-start.2 = ((bf16[16,192,640]{2,1,0:T(8,128)(2,1)}), bf16[16,192,640]{2,1,0:T(8,128)(2,1)}, u32[]{:S(2)}, u32[]{:S(2)}) async-start(bf16[16,192,640]{2,1,0:T(8,128)(2,1)} %pad_maximum_fusion), calls=%async_computation.2 | async-start | bytes 7864320 | tf_op jit(solution)/shard_map/all_to_all | solution.py:125
  116.1 3.7 %copy-start.2 = (bf16[2048,640]{1,0:T(8,128)(2,1)S(1)}, bf16[2048,640]{1,0:T(8,128)(2,1)}, u32[]{:S(2)}) copy-start(bf16[2048,640]{1,0:T(8,128)(2,1)} %copy-done.1) | copy-start | bytes 7864324
  119.1 0.7 copy-start.6
  122.0 30.0 %collective-permute-start.3 = (bf16[384,640]{1,0:T(8,128)(2,1)S(1)}, bf16[384,640]{1,0:T(8,128)(2,1)S(1)}, u32[]{:S(2)}, u32[]{:S(2)}) collective-permute-start(bf16[384,640]{1,0:T(8,128)(2,1)S(1)} %pad_maximum_fusion.6), channel_id=1, source_target_pairs={{0,1},{1,0},{2,3},{3,2},{4,7},{5,6},{6,5},{7,4},{8,9},{9,8},{10,11... | collective-permute-start | bytes 1474568 | tf_op jit(solution)/shard_map/ppermute | solution.py:138
  153.1 25.3 %collective-permute-start.4 = (bf16[320,640]{1,0:T(8,128)(2,1)S(1)}, bf16[320,640]{1,0:T(8,128)(2,1)S(1)}, u32[]{:S(2)}, u32[]{:S(2)}) collective-permute-start(bf16[320,640]{1,0:T(8,128)(2,1)S(1)} %pad_maximum_fusion.7), channel_id=1, source_target_pairs={{0,3},{1,2},{2,1},{3,0},{4,5},{5,4},{6,7},{7,6},{8,11},{9,10},{10,... | collective-permute-start | bytes 1228808 | tf_op jit(solution)/shard_map/ppermute | solution.py:138

commit v4 on v3

--- a/solution.py
+++ b/solution.py
@@ -106,9 +106,15 @@
     weights = gathered.reshape(n_tok, 2, own, feats) * keep_both[:, :, None, :]
     weights = weights.reshape(2 * units, feats)
     both_half = sum_cores(dot(tokens, weights, 1, 1))
-    parts = lax.all_to_all(
-        jnp.concatenate([both_half, grad_half], axis=2), "hid", 0, 0, axis_index_groups=lines
-    )
+    def trade(value, by_core):
+        return lax.ppermute(value, "hid", [(i, i ^ (2 * by_core[i % 2])) for i in range(n_hid)])
+
+    z = h // 2
+    halves = jnp.concatenate([both_half, grad_half], axis=2)
+    near, far = z ^ jnp.where(c == 0, 2, 1), z ^ jnp.where(c == 0, 1, 2)
+    got = trade(jnp.stack([pick(halves, near), pick(halves, z ^ 3)]), (2, 1))
+    sent_sum = (pick(halves, far).astype(F32) + got[1].astype(F32)).astype(BF)
+    parts = jnp.stack([pick(halves, z), got[0], trade(sent_sum, (1, 2))])
     acts = activation(own, units, parts)
     mine = lax.all_gather(acts, "hid", axis=0, tiled=True, axis_index_groups=lines)
     other = hop_hid(mine, 1)

time: 182 us -> 181 us (level)
  blocking collectives: 66.2 us -> 39.2 us
  starting transfers between devices: 42.7 us -> 57.2 us
  waiting for transfers between devices: 38 us -> 48.7 us
    all_to_all x1 -> x0, blocking collectives: 26.4 us -> none  [body(): lax.all_to_all(jnp.concatenate([both_half, grad_half], axis=2), 'hid', 0,...]
    ppermute x0 -> x2, waiting for transfers between devices: none -> 13.6 us  [trade(): lax.ppermute(value, 'hid', [(i, i ^ 2 * by_core[i % 2]) for i in range(n_...]
    ppermute x0 -> x2, starting transfers between devices: none -> 9.89 us  [trade(): lax.ppermute(value, 'hid', [(i, i ^ 2 * by_core[i % 2]) for i in range(n_...]
    ppermute x2, starting transfers between devices: 17.3 us -> 19.7 us  [swap(): return lax.ppermute(jnp.concatenate(values), ('hid', 'ffn'), perm)]
    ppermute x3, starting transfers between devices: 13.2 us -> 15.2 us  [hop_hid(): return lax.ppermute(value, 'hid', [(i, i ^ distance) for i in range(n_hid)])]
  transfers between devices with their start and end apart: 7 -> 9, of which waited for: 4 -> 6; matrix products, arithmetic and copies ran while one was open for 10% -> 10% of each run, Pallas kernels for 0% -> 0%
where the time goes in v4:
time: 181 us; the launch traced here: 180 us
  starting transfers between devices  57.2 us (32%)
  waiting for transfers between devices  48.7 us (27%)
  blocking collectives  39.2 us (22%)
  other arithmetic  18 us (10%)
  matrix products  8.64 us (5%)
  local copies, waits for them, and re-layouts  6.11 us (3%)
    all_gather x1, blocking collectives, body(): grad_rows = lax.all_gather(cotangent, 'ffn', axis=0, tiled=True)  24.4 us
    ppermute x2, starting transfers between devices, swap(): return lax.ppermute(jnp.concatenate(values), ('hid', 'ffn'), perm)  19.7 us
    ppermute x2, waiting for transfers between devices, swap(): return lax.ppermute(jnp.concatenate(values), ('hid', 'ffn'), perm)  17.8 us
    ppermute x3, starting transfers between devices, hop_hid(): return lax.ppermute(value, 'hid', [(i, i ^ distance) for i in range(n_hid)])  15.2 us
    all_gather x1, blocking collectives, body(): lax.all_gather(acts, 'hid', axis=0, tiled=True, axis_index_groups=lines)  14.8 us
    all_to_all x1, waiting for transfers between devices, body(): lax.all_to_all(jnp.concatenate([delta_term, down_term], axis=1), 'tok', 0...  13.6 us
    ppermute x2, waiting for transfers between devices, trade(): lax.ppermute(value, 'hid', [(i, i ^ 2 * by_core[i % 2]) for i in range(n_...  13.6 us
    ppermute x2, starting transfers between devices, trade(): lax.ppermute(value, 'hid', [(i, i ^ 2 * by_core[i % 2]) for i in range(n_...  9.89 us
  transfers between devices with their start and end apart: 9, of which 6 were waited for; matrix products, arithmetic and copies ran while one was open for 10% of the time, Pallas kernels for 0%

profile of v4, /device:TPU:1, one launch (start us, length us, event | category | flops | bytes accessed | tf_op | source)
XLA Modules:
  0.0 179.9 jit_solution(3530109340672053771)
XLA Ops:
  0.6 1.0 pad_maximum_fusion.11
  1.6 1.8 %broadcast_in_dim.27 = bf16[16,128,640]{2,1,0:T(8,128)(2,1)} broadcast(bf16[128,640]{1,0:T(8,128)(2,1)S(1)} %pad_maximum_fusion.11), dimensions={1,2} | broadcast | bytes 2785280 | tf_op jit(solution)/shard_map/broadcast_in_dim | solution.py:84
  3.4 7.6 %all-to-all-start = ((bf16[16,128,640]{2,1,0:T(8,128)(2,1)}), bf16[16,128,640]{2,1,0:T(8,128)(2,1)S(1)}, u32[]{:S(2)}, u32[]{:S(2)}) async-start(bf16[16,128,640]{2,1,0:T(8,128)(2,1)} %broadcast_in_dim.27), calls=%async_computation | async-start | bytes 5242880 | tf_op jit(solution)/shard_map/all_to_all | solution.py:87
  11.1 0.8 dynamic-slice_convert_fusion.2
  11.9 0.1 copy.14
  12.0 2.5 %bitcast_multiply_fusion.1 = bf16[1024,640]{1,0:T(8,128)(2,1)} fusion(bf16[1024,640]{1,0:T(8,128)(2,1)} %param.11, bf16[8,640]{1,0:T(8,128)(2,1)S(1)} %broadcast_bitcast_fusion.2), kind=kLoop, calls=%fused_computation.6 | loop fusion | flops 655360 | bytes 2631680 | tf_op jit(solution)/shard_map/mul | solution.py:80
  14.6 24.4 %all_gather.6 = bf16[256,640]{1,0:T(8,128)(2,1)S(1)} all-gather(bf16[64,640]{1,0:T(8,128)(2,1)S(1)} %copy-done.9), channel_id=1, replica_groups=mesh['tok'=16,'hid'=8,'ffn'=4] {'ffn'}, dimensions={0}, use_global_device_ids=true | all-gather | bytes 409600 | tf_op jit(solution)/shard_map/all_gather | solution.py:97
  39.0 1.9 %convolution_convert_fusion.3 = bf16[1024,256]{0,1:T(8,128)(2,1)S(1)} fusion(bf16[1024,640]{1,0:T(8,128)(2,1)} %bitcast_multiply_fusion.1, bf16[256,640]{1,0:T(8,128)(2,1)S(1)} %all_gather.6), kind=kOutput, calls=%fused_computation.7 | convolution fusion | flops 335806464 | bytes 2162688 | tf_op jit(solution)/shard_map/dot_general | solution.py:14
  40.9 0.8 copy-done.3
  41.7 5.5 %collective-permute-start = (bf16[128,1024]{1,0:T(8,128)(2,1)S(1)}, bf16[128,1024]{1,0:T(8,128)(2,1)}, u32[]{:S(2)}, u32[]{:S(2)}) collective-permute-start(bf16[128,1024]{1,0:T(8,128)(2,1)S(1)} %dynamic-slice_bitcast_fusion.1), channel_id=1, source_target_pairs={{0,4},{4,0},{8,12},{12,8},{16,20},{20,16},{24,28},{28,24},{1,5},{5... | collective-permute-start | bytes 786440 | tf_op jit(solution)/shard_map/ppermute | solution.py:73
  47.2 0.8 fusion.11
  48.0 0.1 copy.16
  48.1 0.1 copy.15
  48.3 0.6 copy.17
  49.0 1.1 fusion.1
  50.1 0.8 broadcast_in_dim.31
  50.8 0.5 bitcast_multiply_fusion
  51.3 1.0 convolution_convert_fusion.1
  52.4 0.6 copy-done.1
  53.0 1.9 %collective-permute-start.1 = (bf16[128,2048]{1,0:T(8,128)(2,1)S(1)}, bf16[128,2048]{1,0:T(8,128)(2,1)S(1)}, u32[]{:S(2)}, u32[]{:S(2)}) collective-permute-start(bf16[128,2048]{1,0:T(8,128)(2,1)S(1)} %dynamic-slice_bitcast_fusion), channel_id=1, source_target_pairs={{0,4},{4,0},{8,12},{12,8},{16,20},{20,16},{24,28},{28,24},{1,5},{5... | collective-permute-start | bytes 1572872 | tf_op jit(solution)/shard_map/ppermute | solution.py:73
  54.9 1.8 %collective-permute-done.1 = bf16[128,2048]{1,0:T(8,128)(2,1)S(1)} collective-permute-done((bf16[128,2048]{1,0:T(8,128)(2,1)S(1)}, bf16[128,2048]{1,0:T(8,128)(2,1)S(1)}, u32[]{:S(2)}, u32[]{:S(2)}) %collective-permute-start.1) | collective-permute-done | bytes 524320 | tf_op jit(solution)/shard_map/ppermute | solution.py:73
  56.8 0.1 fusion
  57.0 4.9 %collective-permute-start.2 = (bf16[2,32,3072]{2,1,0:T(8,128)(2,1)S(1)}, bf16[2,32,3072]{2,1,0:T(8,128)(2,1)S(1)}, u32[]{:S(2)}, u32[]{:S(2)}) collective-permute-start(bf16[2,32,3072]{2,1,0:T(8,128)(2,1)S(1)} %pad_maximum_fusion.8), channel_id=1, source_target_pairs={{0,16},{4,12},{8,24},{12,4},{16,0},{20,28},{24,8},{28,20},{1,17},{... | collective-permute-start | bytes 1179656 | tf_op jit(solution)/shard_map/ppermute | solution.py:110
  61.9 8.9 %collective-permute-done.2 = bf16[2,32,3072]{2,1,0:T(8,128)(2,1)S(1)} collective-permute-done((bf16[2,32,3072]{2,1,0:T(8,128)(2,1)S(1)}, bf16[2,32,3072]{2,1,0:T(8,128)(2,1)S(1)}, u32[]{:S(2)}, u32[]{:S(2)}) %collective-permute-start.2) | collective-permute-done | bytes 393248 | tf_op jit(solution)/shard_map/ppermute | solution.py:110
  70.9 5.0 %collective-permute-start.3 = (bf16[32,3072]{1,0:T(8,128)(2,1)S(1)}, bf16[32,3072]{1,0:T(8,128)(2,1)S(1)}, u32[]{:S(2)}, u32[]{:S(2)}) collective-permute-start(bf16[32,3072]{1,0:T(8,128)(2,1)S(1)} %fusion.2), channel_id=1, source_target_pairs={{0,8},{4,20},{8,0},{12,28},{16,24},{20,4},{24,16},{28,12},{1,9},{5... | collective-permute-start | bytes 589832 | tf_op jit(solution)/shard_map/ppermute | solution.py:110
  76.0 4.7 %collective-permute-done.3 = bf16[32,3072]{1,0:T(8,128)(2,1)S(1)} collective-permute-done((bf16[32,3072]{1,0:T(8,128)(2,1)S(1)}, bf16[32,3072]{1,0:T(8,128)(2,1)S(1)}, u32[]{:S(2)}, u32[]{:S(2)}) %collective-permute-start.3) | collective-permute-done | bytes 196640 | tf_op jit(solution)/shard_map/ppermute | solution.py:110
  80.7 0.9 shard_map.119
  81.6 14.8 %all_gather.7 = bf16[128,3072]{1,0:T(8,128)(2,1)S(1)} all-gather(bf16[32,3072]{1,0:T(8,128)(2,1)S(1)} %shard_map.119), channel_id=1, replica_groups={{0,8,16,24},{4,12,20,28},{1,9,17,25},{5,13,21,29},{2,10,18,26},{6,14,22..., dimensions={0}, use_global_device_ids=true | all-gather | bytes 983040 | tf_op jit(solution)/shard_map/all_gather | solution.py:119
  96.3 7.8 %collective-permute-start.4 = (bf16[128,3072]{1,0:T(8,128)(2,1)S(1)}, bf16[128,3072]{1,0:T(8,128)(2,1)S(1)}, u32[]{:S(2)}, u32[]{:S(2)}) collective-permute-start(bf16[128,3072]{1,0:T(8,128)(2,1)S(1)} %all_gather.7), channel_id=1, source_target_pairs={{0,4},{4,0},{8,12},{12,8},{16,20},{20,16},{24,28},{28,24},{1,5},{5... | collective-permute-start | bytes 2359304 | tf_op jit(solution)/shard_map/ppermute | solution.py:73
  104.2 1.9 %collective-permute-done.4 = bf16[128,3072]{1,0:T(8,128)(2,1)S(1)} collective-permute-done((bf16[128,3072]{1,0:T(8,128)(2,1)S(1)}, bf16[128,3072]{1,0:T(8,128)(2,1)S(1)}, u32[]{:S(2)}, u32[]{:S(2)}) %collective-permute-start.4) | collective-permute-done | bytes 786464 | tf_op jit(solution)/shard_map/ppermute | solution.py:73
  106.1 0.6 convolution_convert_fusion.2
  106.8 1.0 convolution_convert_fusion
  107.9 2.3 %pad_maximum_fusion = bf16[16,192,640]{2,1,0:T(8,128)(2,1)} fusion(bf16[16,64,640]{2,1,0:T(8,128)(2,1)S(1)} %bitcast.85, bf16[16,128,640]{2,1,0:T(8,128)(2,1)S(1)} %bitcast.82), kind=kLoop, calls=%fused_computation.1 | loop fusion | flops 7864320 | bytes 7864320 | tf_op jit(solution)/shard_map/concatenate | solution.py:131
  110.2 4.8 %all-to-all-start.1 = ((bf16[16,192,640]{2,1,0:T(8,128)(2,1)}), bf16[16,192,640]{2,1,0:T(8,128)(2,1)}, u32[]{:S(2)}, u32[]{:S(2)}) async-start(bf16[16,192,640]{2,1,0:T(8,128)(2,1)} %pad_maximum_fusion), calls=%async_computation.1 | async-start | bytes 7864320 | tf_op jit(solution)/shard_map/all_to_all | solution.py:131
  115.0 0.9 bitcast_convert_fusion
  116.0 1.9 %convolution_convert_fusion.5 = bf16[256,640]{1,0:T(8,128)(2,1)S(1)} fusion(bf16[1024,640]{1,0:T(8,128)(2,1)} %bitcast_multiply_fusion.1, bf16[128,1024]{1,0:T(8,128)(2,1)S(1)} %copy-done.8, bf16[128,1024]{1,0:T(8,128)(2,1)S(1)} %get-tuple-element.15), kind=kOutput, calls=%fused_computation.13 | convolution fusion | flops 336756736 | bytes 2162688 | tf_op jit(solution)/shard_map/dot_general | solution.py:14
  117.9 0.7 copy-done.6
  118.7 2.2 %convolution_convert_fusion.4 = bf16[256,640]{1,0:T(8,128)(2,1)S(1)} fusion(bf16[2048,640]{1,0:T(8,128)(2,1)S(1)} %copy-done.2, bf16[128,2048]{1,0:T(8,128)(2,1)} %copy-done.5, bf16[128,2048]{1,0:T(8,128)(2,1)} %copy-done.4), kind=kOutput, calls=%fused_computation.12 | convolution fusion | flops 673349632 | bytes 3997696 | tf_op jit(solution)/shard_map/dot_general | solution.py:14
  120.9 11.3 %collective-permute-start.5 = (bf16[384,640]{1,0:T(8,128)(2,1)S(1)}, bf16[384,640]{1,0:T(8,128)(2,1)S(1)}, u32[]{:S(2)}, u32[]{:S(2)}) collective-permute-start(bf16[384,640]{1,0:T(8,128)(2,1)S(1)} %pad_maximum_fusion.6), channel_id=1, source_target_pairs={{0,1},{1,0},{2,3},{3,2},{4,7},{5,6},{6,5},{7,4},{8,9},{9,8},{10,11... | collective-permute-start | bytes 1474568 | tf_op jit(solution)/shard_map/ppermute | solution.py:144
  132.2 0.8 bitcast_convert_fusion.1
  133.2 17.8 %collective-permute-done.5 = bf16[384,640]{1,0:T(8,128)(2,1)S(1)} collective-permute-done((bf16[384,640]{1,0:T(8,128)(2,1)S(1)}, bf16[384,640]{1,0:T(8,128)(2,1)S(1)}, u32[]{:S(2)}, u32[]{:S(2)}) %collective-permute-start.5) | collective-permute-done | bytes 491552 | tf_op jit(solution)/shard_map/ppermute | solution.py:144
  151.0 0.9 fusion.7
  152.0 8.4 %collective-permute-start.6 = (bf16[320,640]{1,0:T(8,128)(2,1)S(1)}, bf16[320,640]{1,0:T(8,128)(2,1)S(1)}, u32[]{:S(2)}, u32[]{:S(2)}) collective-permute-start(bf16[320,640]{1,0:T(8,128)(2,1)S(1)} %pad_maximum_fusion.7), channel_id=1, source_target_pairs={{0,3},{1,2},{2,1},{3,0},{4,5},{5,4},{6,7},{7,6},{8,11},{9,10},{10,... | collective-permute-start | bytes 1228808 | tf_op jit(solution)/shard_map/ppermute | solution.py:144
  160.4 13.6 %all-to-all-done.1 = bf16[16,192,640]{2,1,0:T(8,128)(2,1)} async-done(((bf16[16,192,640]{2,1,0:T(8,128)(2,1)}), bf16[16,192,640]{2,1,0:T(8,128)(2,1)}, u32[]{:S(2)}, u32[]{:S(2)}) %all-to-all-start.1) | async-done | bytes 3932192 | tf_op jit(solution)/shard_map/all_to_all | solution.py:131
  174.0 2.7 %convert_reduce_fusion = f32[192,640]{1,0:T(8,128)S(1)} fusion(bf16[16,192,640]{2,1,0:T(8,128)(2,1)} %all-to-all-done.1), kind=kLoop, calls=%fused_computation | loop fusion | flops 3809280 | bytes 4423680 | tf_op jit(solution)/shard_map/reduce_sum | solution.py:20
  176.8 0.8 add_convert_fusion
  177.6 0.7 multiply_convert_fusion
  178.3 1.6 add_convert_fusion.3
  (41 shorter events, 1.1 us)
Async XLA Ops:
  0.6 50.7 %copy-start = (bf16[256,640]{1,0:T(8,128)(2,1)S(1)}, bf16[256,640]{1,0:T(8,128)(2,1)}, u32[]{:S(2)}) copy-start(bf16[256,640]{1,0:T(8,128)(2,1)} %param.8) | copy-start | bytes 983044
  3.4 46.6 %all-to-all-start = ((bf16[16,128,640]{2,1,0:T(8,128)(2,1)}), bf16[16,128,640]{2,1,0:T(8,128)(2,1)S(1)}, u32[]{:S(2)}, u32[]{:S(2)}) async-start(bf16[16,128,640]{2,1,0:T(8,128)(2,1)} %broadcast_in_dim.27), calls=%async_computation | async-start | bytes 5242880 | tf_op jit(solution)/shard_map/all_to_all | solution.py:87
  11.0 3.5 %copy-start.9 = (bf16[64,640]{1,0:T(8,128)(2,1)S(1)}, bf16[64,640]{1,0:T(8,128)(2,1)}, u32[]{:S(2)}) copy-start(bf16[64,640]{1,0:T(8,128)(2,1)} %param.15) | copy-start | bytes 245764
  40.9 0.8 copy-start.3
  41.7 7.2 %collective-permute-start = (bf16[128,1024]{1,0:T(8,128)(2,1)S(1)}, bf16[128,1024]{1,0:T(8,128)(2,1)}, u32[]{:S(2)}, u32[]{:S(2)}) collective-permute-start(bf16[128,1024]{1,0:T(8,128)(2,1)S(1)} %dynamic-slice_bitcast_fusion.1), channel_id=1, source_target_pairs={{0,4},{4,0},{8,12},{12,8},{16,20},{20,16},{24,28},{28,24},{1,5},{5... | collective-permute-start | bytes 786440 | tf_op jit(solution)/shard_map/ppermute | solution.py:73
  51.3 1.6 copy-start.1
  53.0 3.8 %collective-permute-start.1 = (bf16[128,2048]{1,0:T(8,128)(2,1)S(1)}, bf16[128,2048]{1,0:T(8,128)(2,1)S(1)}, u32[]{:S(2)}, u32[]{:S(2)}) collective-permute-start(bf16[128,2048]{1,0:T(8,128)(2,1)S(1)} %dynamic-slice_bitcast_fusion), channel_id=1, source_target_pairs={{0,4},{4,0},{8,12},{12,8},{16,20},{20,16},{24,28},{28,24},{1,5},{5... | collective-permute-start | bytes 1572872 | tf_op jit(solution)/shard_map/ppermute | solution.py:73
  57.0 13.8 %collective-permute-start.2 = (bf16[2,32,3072]{2,1,0:T(8,128)(2,1)S(1)}, bf16[2,32,3072]{2,1,0:T(8,128)(2,1)S(1)}, u32[]{:S(2)}, u32[]{:S(2)}) collective-permute-start(bf16[2,32,3072]{2,1,0:T(8,128)(2,1)S(1)} %pad_maximum_fusion.8), channel_id=1, source_target_pairs={{0,16},{4,12},{8,24},{12,4},{16,0},{20,28},{24,8},{28,20},{1,17},{... | collective-permute-start | bytes 1179656 | tf_op jit(solution)/shard_map/ppermute | solution.py:110
  70.9 9.7 %collective-permute-start.3 = (bf16[32,3072]{1,0:T(8,128)(2,1)S(1)}, bf16[32,3072]{1,0:T(8,128)(2,1)S(1)}, u32[]{:S(2)}, u32[]{:S(2)}) collective-permute-start(bf16[32,3072]{1,0:T(8,128)(2,1)S(1)} %fusion.2), channel_id=1, source_target_pairs={{0,8},{4,20},{8,0},{12,28},{16,24},{20,4},{24,16},{28,12},{1,9},{5... | collective-permute-start | bytes 589832 | tf_op jit(solution)/shard_map/ppermute | solution.py:110
  96.3 9.7 %collective-permute-start.4 = (bf16[128,3072]{1,0:T(8,128)(2,1)S(1)}, bf16[128,3072]{1,0:T(8,128)(2,1)S(1)}, u32[]{:S(2)}, u32[]{:S(2)}) collective-permute-start(bf16[128,3072]{1,0:T(8,128)(2,1)S(1)} %all_gather.7), channel_id=1, source_target_pairs={{0,4},{4,0},{8,12},{12,8},{16,20},{20,16},{24,28},{28,24},{1,5},{5... | collective-permute-start | bytes 2359304 | tf_op jit(solution)/shard_map/ppermute | solution.py:73
  106.1 1.8 copy-start.7
  106.8 1.1 copy-start.4
  106.8 1.1 copy-start.5
  110.2 5.8 %copy-start.8 = (bf16[128,1024]{1,0:T(8,128)(2,1)S(1)}, bf16[128,1024]{1,0:T(8,128)(2,1)}, u32[]{:S(2)}) copy-start(bf16[128,1024]{1,0:T(8,128)(2,1)} %copy-done.7) | copy-start | bytes 786436
  110.2 63.8 %all-to-all-start.1 = ((bf16[16,192,640]{2,1,0:T(8,128)(2,1)}), bf16[16,192,640]{2,1,0:T(8,128)(2,1)}, u32[]{:S(2)}, u32[]{:S(2)}) async-start(bf16[16,192,640]{2,1,0:T(8,128)(2,1)} %pad_maximum_fusion), calls=%async_computation.1 | async-start | bytes 7864320 | tf_op jit(solution)/shard_map/all_to_all | solution.py:131
  115.0 3.7 %copy-start.2 = (bf16[2048,640]{1,0:T(8,128)(2,1)S(1)}, bf16[2048,640]{1,0:T(8,128)(2,1)}, u32[]{:S(2)}) copy-start(bf16[2048,640]{1,0:T(8,128)(2,1)} %copy-done.1) | copy-start | bytes 7864324
  117.9 0.7 copy-start.6
  120.9 30.1 %collective-permute-start.5 = (bf16[384,640]{1,0:T(8,128)(2,1)S(1)}, bf16[384,640]{1,0:T(8,128)(2,1)S(1)}, u32[]{:S(2)}, u32[]{:S(2)}) collective-permute-start(bf16[384,640]{1,0:T(8,128)(2,1)S(1)} %pad_maximum_fusion.6), channel_id=1, source_target_pairs={{0,1},{1,0},{2,3},{3,2},{4,7},{5,6},{6,5},{7,4},{8,9},{9,8},{10,11... | collective-permute-start | bytes 1474568 | tf_op jit(solution)/shard_map/ppermute | solution.py:144
  152.0 24.8 %collective-permute-start.6 = (bf16[320,640]{1,0:T(8,128)(2,1)S(1)}, bf16[320,640]{1,0:T(8,128)(2,1)S(1)}, u32[]{:S(2)}, u32[]{:S(2)}) collective-permute-start(bf16[320,640]{1,0:T(8,128)(2,1)S(1)} %pad_maximum_fusion.7), channel_id=1, source_target_pairs={{0,3},{1,2},{2,1},{3,0},{4,5},{5,4},{6,7},{7,6},{8,11},{9,10},{10,... | collective-permute-start | bytes 1228808 | tf_op jit(solution)/shard_map/ppermute | solution.py:144

commit v5 on v4

--- a/solution.py
+++ b/solution.py
@@ -129,7 +129,12 @@
     delta_term = dot(deltas, tokens, 0, 0).astype(BF).reshape(n_tok, 2 * own, feats)
     down_term = dot(hidden, grad_rows, 0, 0).astype(BF).reshape(n_tok, own, feats)
     terms = lax.all_to_all(jnp.concatenate([delta_term, down_term], axis=1), "tok", 0, 0)
-    sums = total(terms) * (1.0 / n_tok)
+
+    def gradient(kind, keep):
+        own_terms = terms[:, kind * own : (kind + 1) * own]
+        return (total(own_terms) * (1.0 / n_tok) * keep.astype(F32)).astype(BF)
+
+    grads = [gradient(k, keep) for k, keep in enumerate((keep_gate, keep_up, keep_own_down))]
 
     def beside(i):
         return i ^ 1
@@ -157,14 +162,12 @@
     own_sum = plus(pick(mixed_part, f), got[rows : rows + block])
     sent_sum = plus(pick(mixed_part, second), got[rows + block :])
     got = swap([input_sum, sent_sum], (around, beside))
-    got, sums = lax.optimization_barrier((got, sums))
+    got, grads = lax.optimization_barrier((got, grads))
     tokens_grad = plus(input_sum, got[:rows])
     mixed = plus(own_sum, got[rows:])
 
-    gate_grad = (sums[:own] * keep_gate.astype(F32)).astype(BF).T
-    up_grad = (sums[own : 2 * own] * keep_up.astype(F32)).astype(BF).T
-    down_grad = (sums[2 * own :] * keep_own_down.astype(F32)).astype(BF)
-    return (mixed, tokens_grad, gate_grad, up_grad, down_grad)
+    gate_grad, up_grad, down_grad = grads
+    return (mixed, tokens_grad, gate_grad.T, up_grad.T, down_grad)
 
 
 def solution(mesh):

time: 181 us -> 182 us (level)
  transfers between devices with their start and end apart: 9 -> 9, of which waited for: 6 -> 6; matrix products, arithmetic and copies ran while one was open for 10% -> 11% of each run, Pallas kernels for 0% -> 0%
where the time goes in v5:
time: 182 us; the launch traced here: 181 us
  starting transfers between devices  57.1 us (31%)
  waiting for transfers between devices  48.7 us (27%)
  blocking collectives  39.2 us (22%)
  other arithmetic  19.2 us (11%)
  matrix products  8.64 us (5%)
  local copies, waits for them, and re-layouts  6.09 us (3%)
    all_gather x1, blocking collectives, body(): grad_rows = lax.all_gather(cotangent, 'ffn', axis=0, tiled=True)  24.4 us
    ppermute x2, starting transfers between devices, swap(): return lax.ppermute(jnp.concatenate(values), ('hid', 'ffn'), perm)  19.7 us
    ppermute x2, waiting for transfers between devices, swap(): return lax.ppermute(jnp.concatenate(values), ('hid', 'ffn'), perm)  17.8 us
    ppermute x3, starting transfers between devices, hop_hid(): return lax.ppermute(value, 'hid', [(i, i ^ distance) for i in range(n_hid)])  15.2 us
    all_gather x1, blocking collectives, body(): lax.all_gather(acts, 'hid', axis=0, tiled=True, axis_index_groups=lines)  14.8 us
    all_to_all x1, waiting for transfers between devices, body(): lax.all_to_all(jnp.concatenate([delta_term, down_term], axis=1), 'tok', 0...  13.6 us
    ppermute x2, waiting for transfers between devices, trade(): lax.ppermute(value, 'hid', [(i, i ^ 2 * by_core[i % 2]) for i in range(n_...  13.6 us
    ppermute x2, starting transfers between devices, trade(): lax.ppermute(value, 'hid', [(i, i ^ 2 * by_core[i % 2]) for i in range(n_...  9.9 us
  transfers between devices with their start and end apart: 9, of which 6 were waited for; matrix products, arithmetic and copies ran while one was open for 11% of the time, Pallas kernels for 0%

profile of v5, /device:TPU:1, one launch (start us, length us, event | category | flops | bytes accessed | tf_op | source)
XLA Modules:
  0.0 181.0 jit_solution(5146653592543037005)
XLA Ops:
  0.6 1.0 pad_maximum_fusion.11
  1.6 1.8 broadcast_in_dim.27
  3.4 7.6 %all-to-all-start = ((bf16[16,128,640]{2,1,0:T(8,128)(2,1)}), bf16[16,128,640]{2,1,0:T(8,128)(2,1)S(1)}, u32[]{:S(2)}, u32[]{:S(2)}) async-start(bf16[16,128,640]{2,1,0:T(8,128)(2,1)} %broadcast_in_dim.27), calls=%async_computation | async-start | bytes 5242880 | tf_op jit(solution)/shard_map/all_to_all | solution.py:87
  11.1 0.8 dynamic-slice_convert_fusion.2
  11.9 0.1 copy.14
  12.0 2.5 %bitcast_multiply_fusion.1 = bf16[1024,640]{1,0:T(8,128)(2,1)} fusion(bf16[1024,640]{1,0:T(8,128)(2,1)} %param.11, bf16[8,640]{1,0:T(8,128)(2,1)S(1)} %broadcast_bitcast_fusion.2), kind=kLoop, calls=%fused_computation.8 | loop fusion | flops 655360 | bytes 2631680 | tf_op jit(solution)/shard_map/mul | solution.py:80
  14.5 24.4 %all_gather.6 = bf16[256,640]{1,0:T(8,128)(2,1)S(1)} all-gather(bf16[64,640]{1,0:T(8,128)(2,1)S(1)} %copy-done.9), channel_id=1, replica_groups=mesh['tok'=16,'hid'=8,'ffn'=4] {'ffn'}, dimensions={0}, use_global_device_ids=true | all-gather | bytes 409600 | tf_op jit(solution)/shard_map/all_gather | solution.py:97
  39.0 1.9 %convolution_convert_fusion.3 = bf16[1024,256]{0,1:T(8,128)(2,1)S(1)} fusion(bf16[1024,640]{1,0:T(8,128)(2,1)} %bitcast_multiply_fusion.1, bf16[256,640]{1,0:T(8,128)(2,1)S(1)} %all_gather.6), kind=kOutput, calls=%fused_computation.9 | convolution fusion | flops 335806464 | bytes 2162688 | tf_op jit(solution)/shard_map/dot_general | solution.py:14
  40.9 0.8 copy-done.3
  41.7 5.4 %collective-permute-start = (bf16[128,1024]{1,0:T(8,128)(2,1)S(1)}, bf16[128,1024]{1,0:T(8,128)(2,1)}, u32[]{:S(2)}, u32[]{:S(2)}) collective-permute-start(bf16[128,1024]{1,0:T(8,128)(2,1)S(1)} %dynamic-slice_bitcast_fusion.1), channel_id=1, source_target_pairs={{0,4},{4,0},{8,12},{12,8},{16,20},{20,16},{24,28},{28,24},{1,5},{5... | collective-permute-start | bytes 786440 | tf_op jit(solution)/shard_map/ppermute | solution.py:73
  47.2 0.8 fusion.9
  48.3 0.6 copy.17
  48.9 1.1 fusion.1
  50.1 0.8 broadcast_in_dim.31
  50.8 0.5 bitcast_multiply_fusion
  51.3 1.0 convolution_convert_fusion.1
  52.3 0.5 copy-done.1
  52.9 1.9 %collective-permute-start.1 = (bf16[128,2048]{1,0:T(8,128)(2,1)S(1)}, bf16[128,2048]{1,0:T(8,128)(2,1)S(1)}, u32[]{:S(2)}, u32[]{:S(2)}) collective-permute-start(bf16[128,2048]{1,0:T(8,128)(2,1)S(1)} %dynamic-slice_bitcast_fusion), channel_id=1, source_target_pairs={{0,4},{4,0},{8,12},{12,8},{16,20},{20,16},{24,28},{28,24},{1,5},{5... | collective-permute-start | bytes 1572872 | tf_op jit(solution)/shard_map/ppermute | solution.py:73
  54.9 1.8 %collective-permute-done.1 = bf16[128,2048]{1,0:T(8,128)(2,1)S(1)} collective-permute-done((bf16[128,2048]{1,0:T(8,128)(2,1)S(1)}, bf16[128,2048]{1,0:T(8,128)(2,1)S(1)}, u32[]{:S(2)}, u32[]{:S(2)}) %collective-permute-start.1) | collective-permute-done | bytes 524320 | tf_op jit(solution)/shard_map/ppermute | solution.py:73
  56.8 0.1 fusion
  57.0 4.9 %collective-permute-start.2 = (bf16[2,32,3072]{2,1,0:T(8,128)(2,1)S(1)}, bf16[2,32,3072]{2,1,0:T(8,128)(2,1)S(1)}, u32[]{:S(2)}, u32[]{:S(2)}) collective-permute-start(bf16[2,32,3072]{2,1,0:T(8,128)(2,1)S(1)} %pad_maximum_fusion.8), channel_id=1, source_target_pairs={{0,16},{4,12},{8,24},{12,4},{16,0},{20,28},{24,8},{28,20},{1,17},{... | collective-permute-start | bytes 1179656 | tf_op jit(solution)/shard_map/ppermute | solution.py:110
  61.9 8.9 %collective-permute-done.2 = bf16[2,32,3072]{2,1,0:T(8,128)(2,1)S(1)} collective-permute-done((bf16[2,32,3072]{2,1,0:T(8,128)(2,1)S(1)}, bf16[2,32,3072]{2,1,0:T(8,128)(2,1)S(1)}, u32[]{:S(2)}, u32[]{:S(2)}) %collective-permute-start.2) | collective-permute-done | bytes 393248 | tf_op jit(solution)/shard_map/ppermute | solution.py:110
  70.9 5.0 %collective-permute-start.3 = (bf16[32,3072]{1,0:T(8,128)(2,1)S(1)}, bf16[32,3072]{1,0:T(8,128)(2,1)S(1)}, u32[]{:S(2)}, u32[]{:S(2)}) collective-permute-start(bf16[32,3072]{1,0:T(8,128)(2,1)S(1)} %fusion.2), channel_id=1, source_target_pairs={{0,8},{4,20},{8,0},{12,28},{16,24},{20,4},{24,16},{28,12},{1,9},{5... | collective-permute-start | bytes 589832 | tf_op jit(solution)/shard_map/ppermute | solution.py:110
  75.9 4.7 %collective-permute-done.3 = bf16[32,3072]{1,0:T(8,128)(2,1)S(1)} collective-permute-done((bf16[32,3072]{1,0:T(8,128)(2,1)S(1)}, bf16[32,3072]{1,0:T(8,128)(2,1)S(1)}, u32[]{:S(2)}, u32[]{:S(2)}) %collective-permute-start.3) | collective-permute-done | bytes 196640 | tf_op jit(solution)/shard_map/ppermute | solution.py:110
  80.7 0.9 shard_map.119
  81.5 14.8 %all_gather.7 = bf16[128,3072]{1,0:T(8,128)(2,1)S(1)} all-gather(bf16[32,3072]{1,0:T(8,128)(2,1)S(1)} %shard_map.119), channel_id=1, replica_groups={{0,8,16,24},{4,12,20,28},{1,9,17,25},{5,13,21,29},{2,10,18,26},{6,14,22..., dimensions={0}, use_global_device_ids=true | all-gather | bytes 983040 | tf_op jit(solution)/shard_map/all_gather | solution.py:119
  96.3 7.8 %collective-permute-start.4 = (bf16[128,3072]{1,0:T(8,128)(2,1)S(1)}, bf16[128,3072]{1,0:T(8,128)(2,1)S(1)}, u32[]{:S(2)}, u32[]{:S(2)}) collective-permute-start(bf16[128,3072]{1,0:T(8,128)(2,1)S(1)} %all_gather.7), channel_id=1, source_target_pairs={{0,4},{4,0},{8,12},{12,8},{16,20},{20,16},{24,28},{28,24},{1,5},{5... | collective-permute-start | bytes 2359304 | tf_op jit(solution)/shard_map/ppermute | solution.py:73
  104.1 1.9 %collective-permute-done.4 = bf16[128,3072]{1,0:T(8,128)(2,1)S(1)} collective-permute-done((bf16[128,3072]{1,0:T(8,128)(2,1)S(1)}, bf16[128,3072]{1,0:T(8,128)(2,1)S(1)}, u32[]{:S(2)}, u32[]{:S(2)}) %collective-permute-start.4) | collective-permute-done | bytes 786464 | tf_op jit(solution)/shard_map/ppermute | solution.py:73
  106.1 0.6 convolution_convert_fusion.2
  106.8 1.0 convolution_convert_fusion
  107.9 2.3 %pad_maximum_fusion = bf16[16,192,640]{2,1,0:T(8,128)(2,1)} fusion(bf16[16,64,640]{2,1,0:T(8,128)(2,1)S(1)} %bitcast.80, bf16[16,128,640]{2,1,0:T(8,128)(2,1)S(1)} %bitcast.77), kind=kLoop, calls=%fused_computation | loop fusion | flops 7864320 | bytes 7864320 | tf_op jit(solution)/shard_map/concatenate | solution.py:131
  110.2 4.8 %all-to-all-start.1 = ((bf16[16,192,640]{2,1,0:T(8,128)(2,1)}), bf16[16,192,640]{2,1,0:T(8,128)(2,1)}, u32[]{:S(2)}, u32[]{:S(2)}) async-start(bf16[16,192,640]{2,1,0:T(8,128)(2,1)} %pad_maximum_fusion), calls=%async_computation.1 | async-start | bytes 7864320 | tf_op jit(solution)/shard_map/all_to_all | solution.py:131
  115.0 0.9 multiply_bitcast_fusion.1
  116.0 1.9 %convolution_convert_fusion.5 = bf16[256,640]{1,0:T(8,128)(2,1)S(1)} fusion(bf16[1024,640]{1,0:T(8,128)(2,1)} %bitcast_multiply_fusion.1, bf16[128,1024]{1,0:T(8,128)(2,1)S(1)} %copy-done.8, bf16[128,1024]{1,0:T(8,128)(2,1)S(1)} %get-tuple-element.22), kind=kOutput, calls=%fused_computation.15 | convolution fusion | flops 336756736 | bytes 2162688 | tf_op jit(solution)/shard_map/dot_general | solution.py:14
  117.9 0.7 copy-done.6
  118.7 2.2 %convolution_convert_fusion.4 = bf16[256,640]{1,0:T(8,128)(2,1)S(1)} fusion(bf16[2048,640]{1,0:T(8,128)(2,1)S(1)} %copy-done.2, bf16[128,2048]{1,0:T(8,128)(2,1)} %copy-done.5, bf16[128,2048]{1,0:T(8,128)(2,1)} %copy-done.4), kind=kOutput, calls=%fused_computation.14 | convolution fusion | flops 673349632 | bytes 3997696 | tf_op jit(solution)/shard_map/dot_general | solution.py:14
  120.9 11.3 %collective-permute-start.5 = (bf16[384,640]{1,0:T(8,128)(2,1)S(1)}, bf16[384,640]{1,0:T(8,128)(2,1)S(1)}, u32[]{:S(2)}, u32[]{:S(2)}) collective-permute-start(bf16[384,640]{1,0:T(8,128)(2,1)S(1)} %pad_maximum_fusion.6), channel_id=1, source_target_pairs={{0,1},{1,0},{2,3},{3,2},{4,7},{5,6},{6,5},{7,4},{8,9},{9,8},{10,11... | collective-permute-start | bytes 1474568 | tf_op jit(solution)/shard_map/ppermute | solution.py:149
  132.2 0.8 multiply_bitcast_fusion
  133.1 17.8 %collective-permute-done.5 = bf16[384,640]{1,0:T(8,128)(2,1)S(1)} collective-permute-done((bf16[384,640]{1,0:T(8,128)(2,1)S(1)}, bf16[384,640]{1,0:T(8,128)(2,1)S(1)}, u32[]{:S(2)}, u32[]{:S(2)}) %collective-permute-start.5) | collective-permute-done | bytes 491552 | tf_op jit(solution)/shard_map/ppermute | solution.py:149
  150.9 0.9 fusion.7
  152.0 8.4 %collective-permute-start.6 = (bf16[320,640]{1,0:T(8,128)(2,1)S(1)}, bf16[320,640]{1,0:T(8,128)(2,1)S(1)}, u32[]{:S(2)}, u32[]{:S(2)}) collective-permute-start(bf16[320,640]{1,0:T(8,128)(2,1)S(1)} %pad_maximum_fusion.7), channel_id=1, source_target_pairs={{0,3},{1,2},{2,1},{3,0},{4,5},{5,4},{6,7},{7,6},{8,11},{9,10},{10,... | collective-permute-start | bytes 1228808 | tf_op jit(solution)/shard_map/ppermute | solution.py:149
  160.4 13.6 %all-to-all-done.1 = bf16[16,192,640]{2,1,0:T(8,128)(2,1)} async-done(((bf16[16,192,640]{2,1,0:T(8,128)(2,1)}), bf16[16,192,640]{2,1,0:T(8,128)(2,1)}, u32[]{:S(2)}, u32[]{:S(2)}) %all-to-all-start.1) | async-done | bytes 3932192 | tf_op jit(solution)/shard_map/all_to_all | solution.py:131
  174.0 2.7 %convert_reduce_fusion = (f32[64,640]{1,0:T(8,128)S(1)}, f32[64,640]{1,0:T(8,128)S(1)}, f32[64,640]{1,0:T(8,128)S(1)}) fusion(bf16[16,192,640]{2,1,0:T(8,128)(2,1)} %all-to-all-done.1), kind=kLoop, calls=%fused_computation.3 | loop fusion | flops 3809280 | bytes 4423680 | tf_op jit(solution)/shard_map/reduce_sum | solution.py:20
  176.7 0.7 multiply_convert_fusion.2
  177.4 0.6 multiply_convert_fusion.1
  178.0 0.7 multiply_convert_fusion
  178.7 0.8 add_convert_fusion
  179.5 1.6 add_convert_fusion.3
  (42 shorter events, 1.3 us)
Async XLA Ops:
  0.6 50.7 %copy-start = (bf16[256,640]{1,0:T(8,128)(2,1)S(1)}, bf16[256,640]{1,0:T(8,128)(2,1)}, u32[]{:S(2)}) copy-start(bf16[256,640]{1,0:T(8,128)(2,1)} %param.8) | copy-start | bytes 983044
  3.4 46.6 %all-to-all-start = ((bf16[16,128,640]{2,1,0:T(8,128)(2,1)}), bf16[16,128,640]{2,1,0:T(8,128)(2,1)S(1)}, u32[]{:S(2)}, u32[]{:S(2)}) async-start(bf16[16,128,640]{2,1,0:T(8,128)(2,1)} %broadcast_in_dim.27), calls=%async_computation | async-start | bytes 5242880 | tf_op jit(solution)/shard_map/all_to_all | solution.py:87
  11.0 3.5 %copy-start.9 = (bf16[64,640]{1,0:T(8,128)(2,1)S(1)}, bf16[64,640]{1,0:T(8,128)(2,1)}, u32[]{:S(2)}) copy-start(bf16[64,640]{1,0:T(8,128)(2,1)} %param.15) | copy-start | bytes 245764
  40.9 0.8 copy-start.3
  41.7 7.2 %collective-permute-start = (bf16[128,1024]{1,0:T(8,128)(2,1)S(1)}, bf16[128,1024]{1,0:T(8,128)(2,1)}, u32[]{:S(2)}, u32[]{:S(2)}) collective-permute-start(bf16[128,1024]{1,0:T(8,128)(2,1)S(1)} %dynamic-slice_bitcast_fusion.1), channel_id=1, source_target_pairs={{0,4},{4,0},{8,12},{12,8},{16,20},{20,16},{24,28},{28,24},{1,5},{5... | collective-permute-start | bytes 786440 | tf_op jit(solution)/shard_map/ppermute | solution.py:73
  51.3 1.6 copy-start.1
  52.9 3.8 %collective-permute-start.1 = (bf16[128,2048]{1,0:T(8,128)(2,1)S(1)}, bf16[128,2048]{1,0:T(8,128)(2,1)S(1)}, u32[]{:S(2)}, u32[]{:S(2)}) collective-permute-start(bf16[128,2048]{1,0:T(8,128)(2,1)S(1)} %dynamic-slice_bitcast_fusion), channel_id=1, source_target_pairs={{0,4},{4,0},{8,12},{12,8},{16,20},{20,16},{24,28},{28,24},{1,5},{5... | collective-permute-start | bytes 1572872 | tf_op jit(solution)/shard_map/ppermute | solution.py:73
  57.0 13.8 %collective-permute-start.2 = (bf16[2,32,3072]{2,1,0:T(8,128)(2,1)S(1)}, bf16[2,32,3072]{2,1,0:T(8,128)(2,1)S(1)}, u32[]{:S(2)}, u32[]{:S(2)}) collective-permute-start(bf16[2,32,3072]{2,1,0:T(8,128)(2,1)S(1)} %pad_maximum_fusion.8), channel_id=1, source_target_pairs={{0,16},{4,12},{8,24},{12,4},{16,0},{20,28},{24,8},{28,20},{1,17},{... | collective-permute-start | bytes 1179656 | tf_op jit(solution)/shard_map/ppermute | solution.py:110
  70.9 9.7 %collective-permute-start.3 = (bf16[32,3072]{1,0:T(8,128)(2,1)S(1)}, bf16[32,3072]{1,0:T(8,128)(2,1)S(1)}, u32[]{:S(2)}, u32[]{:S(2)}) collective-permute-start(bf16[32,3072]{1,0:T(8,128)(2,1)S(1)} %fusion.2), channel_id=1, source_target_pairs={{0,8},{4,20},{8,0},{12,28},{16,24},{20,4},{24,16},{28,12},{1,9},{5... | collective-permute-start | bytes 589832 | tf_op jit(solution)/shard_map/ppermute | solution.py:110
  96.3 9.7 %collective-permute-start.4 = (bf16[128,3072]{1,0:T(8,128)(2,1)S(1)}, bf16[128,3072]{1,0:T(8,128)(2,1)S(1)}, u32[]{:S(2)}, u32[]{:S(2)}) collective-permute-start(bf16[128,3072]{1,0:T(8,128)(2,1)S(1)} %all_gather.7), channel_id=1, source_target_pairs={{0,4},{4,0},{8,12},{12,8},{16,20},{20,16},{24,28},{28,24},{1,5},{5... | collective-permute-start | bytes 2359304 | tf_op jit(solution)/shard_map/ppermute | solution.py:73
  106.1 1.8 copy-start.7
  106.8 1.1 copy-start.4
  106.8 1.1 copy-start.5
  110.2 5.8 %copy-start.8 = (bf16[128,1024]{1,0:T(8,128)(2,1)S(1)}, bf16[128,1024]{1,0:T(8,128)(2,1)}, u32[]{:S(2)}) copy-start(bf16[128,1024]{1,0:T(8,128)(2,1)} %copy-done.7) | copy-start | bytes 786436
  110.2 63.8 %all-to-all-start.1 = ((bf16[16,192,640]{2,1,0:T(8,128)(2,1)}), bf16[16,192,640]{2,1,0:T(8,128)(2,1)}, u32[]{:S(2)}, u32[]{:S(2)}) async-start(bf16[16,192,640]{2,1,0:T(8,128)(2,1)} %pad_maximum_fusion), calls=%async_computation.1 | async-start | bytes 7864320 | tf_op jit(solution)/shard_map/all_to_all | solution.py:131
  114.9 3.7 %copy-start.2 = (bf16[2048,640]{1,0:T(8,128)(2,1)S(1)}, bf16[2048,640]{1,0:T(8,128)(2,1)}, u32[]{:S(2)}) copy-start(bf16[2048,640]{1,0:T(8,128)(2,1)} %copy-done.1) | copy-start | bytes 7864324
  117.9 0.7 copy-start.6
  120.9 30.1 %collective-permute-start.5 = (bf16[384,640]{1,0:T(8,128)(2,1)S(1)}, bf16[384,640]{1,0:T(8,128)(2,1)S(1)}, u32[]{:S(2)}, u32[]{:S(2)}) collective-permute-start(bf16[384,640]{1,0:T(8,128)(2,1)S(1)} %pad_maximum_fusion.6), channel_id=1, source_target_pairs={{0,1},{1,0},{2,3},{3,2},{4,7},{5,6},{6,5},{7,4},{8,9},{9,8},{10,11... | collective-permute-start | bytes 1474568 | tf_op jit(solution)/shard_map/ppermute | solution.py:149
  152.0 26.7 %collective-permute-start.6 = (bf16[320,640]{1,0:T(8,128)(2,1)S(1)}, bf16[320,640]{1,0:T(8,128)(2,1)S(1)}, u32[]{:S(2)}, u32[]{:S(2)}) collective-permute-start(bf16[320,640]{1,0:T(8,128)(2,1)S(1)} %pad_maximum_fusion.7), channel_id=1, source_target_pairs={{0,3},{1,2},{2,1},{3,0},{4,5},{5,4},{6,7},{7,6},{8,11},{9,10},{10,... | collective-permute-start | bytes 1228808 | tf_op jit(solution)/shard_map/ppermute | solution.py:149
